TPU v7x, 128 devices: a whole 4x4x4 slice. The times are simulated.
128 devices in a mesh: docs: 128 (over y, x, z, core).
Axes of the slice: x: 4, y: 4, z: 4, core: 2. Of those that a mesh axis runs over, the one named last changes fastest.
Arguments:
- embeddings: bfloat16 [131072, 1024], P('docs'), may hold values from -6 to 6
- cluster_sizes: int32 [64], replicated, may hold values from 1 to 8192, 131072 in all
Outputs:
- row_best: float32 [131072], P('docs')
- cluster_max: float32 [64], replicated
Inputs may be any that keep to these rules, and one draw needn't show every extreme that they name: `cluster_sizes`: rows of one cluster are consecutive in the sorted order; the sizes add up to 131072 and the largest is exactly 8192.
All inputs are finite; a program needn't handle non-finite values.
Results may differ from a plain program's by a relative error of at most 0.0013.
Values may be sent and summed in bfloat16 or wider, within the bound.
No kernel may reach another device: no remote copies, remote signals or barrier semaphores. Data moves between devices by JAX's collectives and lax.ppermute only.
A program may use at most 128 MiB of HBM per device.

v0:
```python
import jax
import jax.numpy as jnp
from jax import lax
from jax.sharding import PartitionSpec as P

REACH = 8


floor_value = -1e30


def from_behind(block, axis, distance):
    devices = range(lax.axis_size(axis))
    route = [(i - distance, i) for i in devices if i - distance in devices]
    return lax.ppermute(block, axis, route)


def cluster_of(cluster_ends, first_row, row_count):
    positions = first_row + jnp.arange(row_count, dtype=jnp.int32)
    found = jnp.sum((cluster_ends[None, :] <= positions[:, None]).astype(jnp.int32), axis=1)
    return (found, positions)


def tile_maxima(left_block, left_ids, left_pos, right_block, right_ids, right_pos, sim_scale):
    scores = (
        lax.dot_general(
            left_block, right_block, (((1,), (1,)), ((), ())), preferred_element_type=jnp.float32
        )
        * sim_scale
    )
    same_cluster = (left_ids[:, None] == right_ids[None, :]) & (
        left_pos[:, None] != right_pos[None, :]
    )
    masked = jnp.where(same_cluster, scores, floor_value)
    return (jnp.max(masked, axis=1), jnp.max(masked, axis=0))


def block_maxima(left_block, left_ids, left_pos, right_block, right_ids, right_pos, sim_scale):
    return tile_maxima(left_block, left_ids, left_pos, right_block, right_ids, right_pos, sim_scale)


def local(embeddings, cluster_sizes):
    row_count = embeddings.shape[0]
    feat_width = embeddings.shape[1]
    sim_scale = 1.0 / feat_width
    own_index = lax.axis_index("docs")
    values = embeddings.astype(jnp.float32)
    normed = (values * lax.rsqrt(jnp.mean(values * values, axis=1, keepdims=True) + 1e-06)).astype(
        jnp.bfloat16
    )
    cluster_ends = jnp.cumsum(cluster_sizes)
    own_ids, own_pos = cluster_of(cluster_ends, own_index * row_count, row_count)
    row_best, unused_cols = block_maxima(
        normed, own_ids, own_pos, normed, own_ids, own_pos, sim_scale
    )
    for distance in range(1, REACH + 1):
        partner = from_behind(normed, "docs", distance)
        partner_ids, partner_pos = cluster_of(
            cluster_ends, (own_index - distance) * row_count, row_count
        )
        partner_ids = jnp.where(own_index >= distance, partner_ids, -1)
        found_mine, found_theirs = block_maxima(
            normed, own_ids, own_pos, partner, partner_ids, partner_pos, sim_scale
        )
        returned = from_behind(jnp.maximum(found_theirs, 0.0), "docs", -distance)
        row_best = jnp.maximum(row_best, jnp.maximum(found_mine, returned))
    row_best = jnp.maximum(row_best, 0.0)
    cluster_bins = jnp.arange(cluster_sizes.shape[0], dtype=jnp.int32)
    in_cluster = own_ids[:, None] == cluster_bins[None, :]
    local_peaks = jnp.max(jnp.where(in_cluster, row_best[:, None], 0.0), axis=0)
    cluster_max = lax.pmax(local_peaks, "docs")
    return (row_best, cluster_max)


def solution(mesh):
    placed = (P("docs", None), P())
    return jax.shard_map(
        local, mesh=mesh, in_specs=placed, out_specs=(P("docs"), P()), check_vma=False
    )
```

profile of v0, /device:TPU:1, one launch (start us, length us, event | category | flops | bytes accessed | tf_op | source)
XLA Modules:
  0.0 526.2 jit_solution(5799484786083423173)
XLA Ops:
  4.7 5.9 %collective-permute-start.12 = (bf16[1024,1024]{1,0:T(8,128)(2,1)S(1)}, bf16[1024,1024]{1,0:T(8,128)(2,1)}, u32[]{:S(2)}, u32[]{:S(2)}) collective-permute-start(bf16[1024,1024]{1,0:T(8,128)(2,1)S(1)} %fusion.1), channel_id=1, source_target_pairs={{0,7},{1,8},{2,9},{3,10},{4,11},{5,12},{6,13},{7,14},{8,15},{9,16}... | collective-permute-start | bytes 6291464 | tf_op jit(solution)/shard_map/ppermute | solution.py:15
  10.6 3.1 collective-permute-start.14
  13.7 7.0 %collective-permute-start.10 = (bf16[1024,1024]{1,0:T(8,128)(2,1)S(1)}, bf16[1024,1024]{1,0:T(8,128)(2,1)}, u32[]{:S(2)}, u32[]{:S(2)}) collective-permute-start(bf16[1024,1024]{1,0:T(8,128)(2,1)S(1)} %fusion.1), channel_id=1, source_target_pairs={{0,6},{1,7},{2,8},{3,9},{4,10},{5,11},{6,12},{7,13},{8,14},{9,15},... | collective-permute-start | bytes 6291464 | tf_op jit(solution)/shard_map/ppermute | solution.py:15
  23.3 2.7 collective-permute-start.4
  26.8 21.8 %collective-permute-done.12 = bf16[1024,1024]{1,0:T(8,128)(2,1)} collective-permute-done((bf16[1024,1024]{1,0:T(8,128)(2,1)S(1)}, bf16[1024,1024]{1,0:T(8,128)(2,1)}, u32[]{:S(2)}, u32[]{:S(2)}) %collective-permute-start.12) | collective-permute-done | bytes 2097184 | tf_op jit(solution)/shard_map/ppermute | solution.py:15
  48.6 11.6 %collective-permute-start.6 = (bf16[1024,1024]{1,0:T(8,128)(2,1)S(1)}, bf16[1024,1024]{1,0:T(8,128)(2,1)S(1)}, u32[]{:S(2)}, u32[]{:S(2)}) collective-permute-start(bf16[1024,1024]{1,0:T(8,128)(2,1)S(1)} %fusion.1), channel_id=1, source_target_pairs={{0,4},{1,5},{2,6},{3,7},{4,8},{5,9},{6,10},{7,11},{8,12},{9,13},{1... | collective-permute-start | bytes 6291464 | tf_op jit(solution)/shard_map/ppermute | solution.py:15
  60.2 4.0 fusion.22
  64.2 13.0 %collective-permute-done.14 = bf16[1024,1024]{1,0:T(8,128)(2,1)} collective-permute-done((bf16[1024,1024]{1,0:T(8,128)(2,1)S(1)}, bf16[1024,1024]{1,0:T(8,128)(2,1)}, u32[]{:S(2)}, u32[]{:S(2)}) %collective-permute-start.14) | collective-permute-done | bytes 2097184 | tf_op jit(solution)/shard_map/ppermute | solution.py:15
  77.1 28.2 %collective-permute-start.8 = (bf16[1024,1024]{1,0:T(8,128)(2,1)S(1)}, bf16[1024,1024]{1,0:T(8,128)(2,1)S(1)}, u32[]{:S(2)}, u32[]{:S(2)}) collective-permute-start(bf16[1024,1024]{1,0:T(8,128)(2,1)S(1)} %fusion.1), channel_id=1, source_target_pairs={{0,5},{1,6},{2,7},{3,8},{4,9},{5,10},{6,11},{7,12},{8,13},{9,14},{... | collective-permute-start | bytes 6291464 | tf_op jit(solution)/shard_map/ppermute | solution.py:15
  105.4 4.0 fusion.23
  109.4 45.3 %collective-permute-done.10 = bf16[1024,1024]{1,0:T(8,128)(2,1)} collective-permute-done((bf16[1024,1024]{1,0:T(8,128)(2,1)S(1)}, bf16[1024,1024]{1,0:T(8,128)(2,1)}, u32[]{:S(2)}, u32[]{:S(2)}) %collective-permute-start.10) | collective-permute-done | bytes 2097184 | tf_op jit(solution)/shard_map/ppermute | solution.py:15
  156.6 6.4 %fusion.12 = (f32[1024]{0:T(1024)S(1)}, f32[1024]{0:T(1024)S(1)}, f32[1024]{0:T(1024)S(1)}, f32[1024]{0:T(1024)S(1)}, f32[1024]{0:T(1024)S(1)}, /*index=5*/f32[1024]{0:T(1024)S(1)}) fusion(s32[1024]{0:T(1024)S(1)} %iota_add_fusion.8, s32[1024]{0:T(1024)S(1)} %get-tuple-element.38, s32[1024]{0:T(1024)S(1)} %iota_add_fusion.2, ...), kind=kOutput, calls=%fused_computation.23 | convolution fusion | flops 2169497600 | bytes 12640256 | tf_op jit(solution)/shard_map/dot_general | solution.py:26
  164.4 4.0 fusion.18
  169.8 4.0 fusion.19
  177.5 14.5 %collective-permute-done.8 = bf16[1024,1024]{1,0:T(8,128)(2,1)S(1)} collective-permute-done((bf16[1024,1024]{1,0:T(8,128)(2,1)S(1)}, bf16[1024,1024]{1,0:T(8,128)(2,1)S(1)}, u32[]{:S(2)}, u32[]{:S(2)}) %collective-permute-start.8) | collective-permute-done | bytes 2097184 | tf_op jit(solution)/shard_map/ppermute | solution.py:15
  194.5 7.6 %collective-permute-done = bf16[1024,1024]{1,0:T(8,128)(2,1)S(1)} collective-permute-done((bf16[1024,1024]{1,0:T(8,128)(2,1)S(1)}, bf16[1024,1024]{1,0:T(8,128)(2,1)S(1)}, u32[]{:S(2)}, u32[]{:S(2)}) %collective-permute-start) | collective-permute-done | bytes 2097184 | tf_op jit(solution)/shard_map/ppermute | solution.py:15
  202.1 7.7 %fusion.2 = (f32[1024]{0:T(1024)S(1)}, f32[1024]{0:T(1024)S(1)}, f32[1024]{0:T(1024)S(1)}, f32[1024]{0:T(1024)S(1)}, f32[1024]{0:T(1024)S(1)}, /*index=5*/f32[10...) fusion(s32[1024]{0:T(1024)S(1)} %iota_add_fusion.8, ...), kind=kOutput, calls=%fused_computation.13 | convolution fusion | flops 2184173568 | bytes 21061632 | tf_op jit(solution)/shard_map/dot_general | solution.py:26
  212.5 41.1 %collective-permute-done.15 = f32[1024]{0:T(1024)S(1)} collective-permute-done((f32[1024]{0:T(1024)S(1)}, f32[1024]{0:T(1024)S(1)}, u32[]{:S(2)}, u32[]{:S(2)}) %collective-permute-start.15) | collective-permute-done | bytes 4128 | tf_op jit(solution)/shard_map/ppermute | solution.py:15
  254.9 4.9 collective-permute-done.13
  261.0 107.2 %collective-permute-done.11 = f32[1024]{0:T(1024)S(1)} collective-permute-done((f32[1024]{0:T(1024)S(1)}, f32[1024]{0:T(1024)S(1)}, u32[]{:S(2)}, u32[]{:S(2)}) %collective-permute-start.11) | collective-permute-done | bytes 4128 | tf_op jit(solution)/shard_map/ppermute | solution.py:15
  368.3 2.9 collective-permute-start.1
  371.1 2.9 select_reduce_fusion
  374.1 49.6 %collective-permute-done.9 = f32[1024]{0:T(1024)S(1)} collective-permute-done((f32[1024]{0:T(1024)S(1)}, f32[1024]{0:T(1024)S(1)}, u32[]{:S(2)}, u32[]{:S(2)}) %collective-permute-start.9) | collective-permute-done | bytes 4128 | tf_op jit(solution)/shard_map/ppermute | solution.py:15
  423.9 102.2 %pmax.7 = f32[64]{0:T(128)} all-reduce(f32[64]{0:T(128)S(1)} %select_reduce_fusion.1), channel_id=1, replica_groups=mesh['docs'=128] {'docs'}, use_global_device_ids=true, to_apply=%region_29.30 | all-reduce | flops 64 | bytes 512 | tf_op jit(solution)/shard_map/pmax | solution.py:71
  (53 shorter events, 23.6 us)
Async XLA Ops:
  0.6 25.4 %copy-start.1 = (s32[64]{0:T(128)S(1)}, s32[64]{0:T(128)}, u32[]{:S(2)}) copy-start(s32[64]{0:T(128)} %param.3) | copy-start | bytes 772
  4.7 43.9 %collective-permute-start.12 = (bf16[1024,1024]{1,0:T(8,128)(2,1)S(1)}, bf16[1024,1024]{1,0:T(8,128)(2,1)}, u32[]{:S(2)}, u32[]{:S(2)}) collective-permute-start(bf16[1024,1024]{1,0:T(8,128)(2,1)S(1)} %fusion.1), channel_id=1, source_target_pairs={{0,7},{1,8},{2,9},{3,10},{4,11},{5,12},{6,13},{7,14},{8,15},{9,16}... | collective-permute-start | bytes 6291464 | tf_op jit(solution)/shard_map/ppermute | solution.py:15
  10.6 66.6 %collective-permute-start.14 = (bf16[1024,1024]{1,0:T(8,128)(2,1)S(1)}, bf16[1024,1024]{1,0:T(8,128)(2,1)}, u32[]{:S(2)}, u32[]{:S(2)}) collective-permute-start(bf16[1024,1024]{1,0:T(8,128)(2,1)S(1)} %fusion.1), channel_id=1, source_target_pairs={{0,8},{1,9},{2,10},{3,11},{4,12},{5,13},{6,14},{7,15},{8,16},{9,17... | collective-permute-start | bytes 6291464 | tf_op jit(solution)/shard_map/ppermute | solution.py:15
  13.7 141.0 %collective-permute-start.10 = (bf16[1024,1024]{1,0:T(8,128)(2,1)S(1)}, bf16[1024,1024]{1,0:T(8,128)(2,1)}, u32[]{:S(2)}, u32[]{:S(2)}) collective-permute-start(bf16[1024,1024]{1,0:T(8,128)(2,1)S(1)} %fusion.1), channel_id=1, source_target_pairs={{0,6},{1,7},{2,8},{3,9},{4,10},{5,11},{6,12},{7,13},{8,14},{9,15},... | collective-permute-start | bytes 6291464 | tf_op jit(solution)/shard_map/ppermute | solution.py:15
  20.7 142.4 %collective-permute-start.2 = (bf16[1024,1024]{1,0:T(8,128)(2,1)S(1)}, bf16[1024,1024]{1,0:T(8,128)(2,1)}, u32[]{:S(2)}, u32[]{:S(2)}) collective-permute-start(bf16[1024,1024]{1,0:T(8,128)(2,1)S(1)} %fusion.1), channel_id=1, source_target_pairs={{0,2},{1,3},{2,4},{3,5},{4,6},{5,7},{6,8},{7,9},{8,10},{9,11},{10,... | collective-permute-start | bytes 6291464 | tf_op jit(solution)/shard_map/ppermute | solution.py:15
  23.3 145.1 %collective-permute-start.4 = (bf16[1024,1024]{1,0:T(8,128)(2,1)S(1)}, bf16[1024,1024]{1,0:T(8,128)(2,1)}, u32[]{:S(2)}, u32[]{:S(2)}) collective-permute-start(bf16[1024,1024]{1,0:T(8,128)(2,1)S(1)} %fusion.1), channel_id=1, source_target_pairs={{0,3},{1,4},{2,5},{3,6},{4,7},{5,8},{6,9},{7,10},{8,11},{9,12},{10... | collective-permute-start | bytes 6291464 | tf_op jit(solution)/shard_map/ppermute | solution.py:15
  48.6 125.2 %collective-permute-start.6 = (bf16[1024,1024]{1,0:T(8,128)(2,1)S(1)}, bf16[1024,1024]{1,0:T(8,128)(2,1)S(1)}, u32[]{:S(2)}, u32[]{:S(2)}) collective-permute-start(bf16[1024,1024]{1,0:T(8,128)(2,1)S(1)} %fusion.1), channel_id=1, source_target_pairs={{0,4},{1,5},{2,6},{3,7},{4,8},{5,9},{6,10},{7,11},{8,12},{9,13},{1... | collective-permute-start | bytes 6291464 | tf_op jit(solution)/shard_map/ppermute | solution.py:15
  77.1 114.9 %collective-permute-start.8 = (bf16[1024,1024]{1,0:T(8,128)(2,1)S(1)}, bf16[1024,1024]{1,0:T(8,128)(2,1)S(1)}, u32[]{:S(2)}, u32[]{:S(2)}) collective-permute-start(bf16[1024,1024]{1,0:T(8,128)(2,1)S(1)} %fusion.1), channel_id=1, source_target_pairs={{0,5},{1,6},{2,7},{3,8},{4,9},{5,10},{6,11},{7,12},{8,13},{9,14},{... | collective-permute-start | bytes 6291464 | tf_op jit(solution)/shard_map/ppermute | solution.py:15
  154.7 47.4 %collective-permute-start = (bf16[1024,1024]{1,0:T(8,128)(2,1)S(1)}, bf16[1024,1024]{1,0:T(8,128)(2,1)S(1)}, u32[]{:S(2)}, u32[]{:S(2)}) collective-permute-start(bf16[1024,1024]{1,0:T(8,128)(2,1)S(1)} %fusion.1), channel_id=1, source_target_pairs={{0,1},{1,2},{2,3},{3,4},{4,5},{5,6},{6,7},{7,8},{8,9},{9,10},{10,1... | collective-permute-start | bytes 6291464 | tf_op jit(solution)/shard_map/ppermute | solution.py:15
  163.1 90.5 %collective-permute-start.15 = (f32[1024]{0:T(1024)S(1)}, f32[1024]{0:T(1024)S(1)}, u32[]{:S(2)}, u32[]{:S(2)}) collective-permute-start(f32[1024]{0:T(1024)S(1)} %broadcast_maximum_fusion), channel_id=1, source_target_pairs={{8,0},{9,1},{10,2},{11,3},{12,4},{13,5},{14,6},{15,7},{16,8},{17,9... | collective-permute-start | bytes 12296 | tf_op jit(solution)/shard_map/ppermute | solution.py:15
  168.4 91.4 %collective-permute-start.13 = (f32[1024]{0:T(1024)S(1)}, f32[1024]{0:T(1024)S(1)}, u32[]{:S(2)}, u32[]{:S(2)}) collective-permute-start(f32[1024]{0:T(1024)S(1)} %broadcast_maximum_fusion.1), channel_id=1, source_target_pairs={{7,0},{8,1},{9,2},{10,3},{11,4},{12,5},{13,6},{14,7},{15,8},{16,9}... | collective-permute-start | bytes 12296 | tf_op jit(solution)/shard_map/ppermute | solution.py:15
  173.8 194.5 %collective-permute-start.11 = (f32[1024]{0:T(1024)S(1)}, f32[1024]{0:T(1024)S(1)}, u32[]{:S(2)}, u32[]{:S(2)}) collective-permute-start(f32[1024]{0:T(1024)S(1)} %broadcast_maximum_fusion.2), channel_id=1, source_target_pairs={{6,0},{7,1},{8,2},{9,3},{10,4},{11,5},{12,6},{13,7},{14,8},{15,9},... | collective-permute-start | bytes 12296 | tf_op jit(solution)/shard_map/ppermute | solution.py:15
  209.9 213.9 %collective-permute-start.9 = (f32[1024]{0:T(1024)S(1)}, f32[1024]{0:T(1024)S(1)}, u32[]{:S(2)}, u32[]{:S(2)}) collective-permute-start(f32[1024]{0:T(1024)S(1)} %broadcast_maximum_fusion.3), channel_id=1, source_target_pairs={{5,0},{6,1},{7,2},{8,3},{9,4},{10,5},{11,6},{12,7},{13,8},{14,9},{... | collective-permute-start | bytes 12296 | tf_op jit(solution)/shard_map/ppermute | solution.py:15
  211.2 212.6 %collective-permute-start.7 = (f32[1024]{0:T(1024)S(1)}, f32[1024]{0:T(1024)S(1)}, u32[]{:S(2)}, u32[]{:S(2)}) collective-permute-start(f32[1024]{0:T(1024)S(1)} %broadcast_maximum_fusion.4), channel_id=1, source_target_pairs={{4,0},{5,1},{6,2},{7,3},{8,4},{9,5},{10,6},{11,7},{12,8},{13,9},{1... | collective-permute-start | bytes 12296 | tf_op jit(solution)/shard_map/ppermute | solution.py:15
  253.6 170.2 %collective-permute-start.5 = (f32[1024]{0:T(1024)S(1)}, f32[1024]{0:T(1024)S(1)}, u32[]{:S(2)}, u32[]{:S(2)}) collective-permute-start(f32[1024]{0:T(1024)S(1)} %broadcast_maximum_fusion.5), channel_id=1, source_target_pairs={{3,0},{4,1},{5,2},{6,3},{7,4},{8,5},{9,6},{10,7},{11,8},{12,9},{13... | collective-permute-start | bytes 12296 | tf_op jit(solution)/shard_map/ppermute | solution.py:15
  259.7 164.0 %collective-permute-start.3 = (f32[1024]{0:T(1024)S(1)}, f32[1024]{0:T(1024)S(1)}, u32[]{:S(2)}, u32[]{:S(2)}) collective-permute-start(f32[1024]{0:T(1024)S(1)} %broadcast_maximum_fusion.6), channel_id=1, source_target_pairs={{2,0},{3,1},{4,2},{5,3},{6,4},{7,5},{8,6},{9,7},{10,8},{11,9},{12,... | collective-permute-start | bytes 12296 | tf_op jit(solution)/shard_map/ppermute | solution.py:15
  368.3 55.5 %collective-permute-start.1 = (f32[1024]{0:T(1024)S(1)}, f32[1024]{0:T(1024)S(1)}, u32[]{:S(2)}, u32[]{:S(2)}) collective-permute-start(f32[1024]{0:T(1024)S(1)} %broadcast_maximum_fusion.7), channel_id=1, source_target_pairs={{1,0},{2,1},{3,2},{4,3},{5,4},{6,5},{7,6},{8,7},{9,8},{10,9},{11,1... | collective-permute-start | bytes 12296 | tf_op jit(solution)/shard_map/ppermute | solution.py:15
  423.8 102.4 %copy-start = (f32[1024]{0:T(1024)}, f32[1024]{0:T(1024)S(1)}, u32[]{:S(2)}) copy-start(f32[1024]{0:T(1024)S(1)} %maximum_maximum_fusion) | copy-start | bytes 12292
where the time goes:
time: 527 us; the launch traced here: 526 us
  waiting for transfers between devices  305 us (58%)
  blocking collectives  102 us (19%)
  starting transfers between devices  75 us (14%)
  matrix products  37.8 us (7%)
    ppermute x16, waiting for transfers between devices, from_behind(): return lax.ppermute(block, axis, route)  305 us
    pmax x1, blocking collectives, local(): cluster_max = lax.pmax(local_peaks, 'docs')  102 us
    ppermute x16, starting transfers between devices, from_behind(): return lax.ppermute(block, axis, route)  75 us
    dot_general x9, matrix products, tile_maxima(): lax.dot_general(left_block, right_block, (((1,), (1,)), ((), ())), prefer...  37.8 us
  transfers between devices with their start and end apart: 16, of which 9 were waited for; matrix products, arithmetic and copies ran while one was open for 7% of the time, Pallas kernels for 0%

commit v1 on v0

v1 whole, which is shorter than its diff:
```python
import functools

import jax
import jax.numpy as jnp
import numpy as np
from jax import lax
from jax.experimental import pallas as pl
from jax.experimental.pallas import tpu as pltpu
from jax.sharding import PartitionSpec as P

AXIS = "docs"
ROWS = 1024
WIDTH = 1024
RING = 8
SLOTS = 6
PIECE = 128
CHUNKS = (256, 256, 256, 256)

RECEIVED = (
    (2, 6, 8),
    (3, 9, 7),
    (5, -6, 1),
    (-4, 0, -5),
    (6, 11, 13),
    (7, 12, 10),
    (0, -3, 4),
    (1, -1, 14),
)
PASSED = (1, 2, 0, 0, 0, 0, 0, 0)
TILES = (
    ((0, 8), (1, 2), (1, 8), (2, 6), (2, 7), (2, 8), (6, 8), (7, 8)),
    ((0, 3), (0, 6), (1, 3), (1, 9), (3, 6), (3, 7), (3, 9), (6, 9)),
    ((-6, -4), (-6, 1), (-6, 2), (-4, 1), (-4, 3), (1, 5), (2, 5)),
    ((-5, -4), (-5, 0), (-5, 2), (-5, 3), (-4, 0), (-4, 2), (0, 2), (0, 5)),
    ((5, 7), (5, 11), (5, 13), (6, 11), (6, 13), (7, 11), (7, 13), (11, 13)),
    ((4, 12), (5, 6), (5, 10), (5, 12), (6, 10), (6, 12), (7, 10), (7, 12)),
    ((-3, 0), (-3, 1), (0, 4), (0, 7), (1, 4), (1, 7), (4, 6), (4, 7)),
    ((-1, 1), (-1, 6), (-1, 7), (1, 6), (6, 14)),
)


def slot_blocks(kind):
    sibling = kind ^ 1
    return (
        (kind, sibling) + RECEIVED[kind] + (RECEIVED[sibling][PASSED[sibling]],)
    )


def tables():
    blocks = np.array([slot_blocks(k) for k in range(RING)], np.int32)
    own, other = [], []
    for k in range(RING):
        held = slot_blocks(k)
        mine, rest = [], []
        for pair in TILES[k]:
            a, b = sorted(held.index(v) for v in pair)
            if a < 2:
                assert b >= 2
                mine.append((a, b))
            else:
                rest.append((a, b))
        own.append(mine)
        other.append(rest)
    most_own = max(len(v) for v in own)
    most_other = max(len(v) for v in other)

    def pack(lists, most):
        out = np.zeros((RING, 1 + 2 * most), np.int32)
        for k, pairs in enumerate(lists):
            out[k, 0] = len(pairs)
            for i, (a, b) in enumerate(pairs):
                out[k, 1 + 2 * i], out[k, 2 + 2 * i] = a, b
        return out

    return blocks, pack(own, most_own), pack(other, most_other)


BLOCKS, OWN_TILES, OTHER_TILES = tables()


def check_cover():
    seen = set()
    for k in range(RING):
        for a, b in TILES[k]:
            d = abs(a - b)
            assert d <= RING and {a, b} <= set(slot_blocks(k))
            low = min(a, b) % RING
            assert (low, d) not in seen
            seen.add((low, d))
    for low in range(RING):
        for d in range(1, RING + 1):
            assert ((low, d) in seen) != (d == 1 and low % 2 == 0)


check_cover()


def routes(count):
    out = []
    for slot in range(3):
        route = []
        for i in range(count):
            source = i - i % RING + RECEIVED[i % RING][slot]
            route.append((source % count, i))
        out.append(route)
    return out


def norm_kernel(x_ref, out_ref):
    v = x_ref[...].astype(jnp.float32)
    mean = jnp.sum(v * v, axis=1, keepdims=True) * (1.0 / WIDTH)
    out_ref[...] = (v * lax.rsqrt(mean + 1e-06)).astype(jnp.bfloat16)


def normalize(embeddings, first, rows):
    step = first // rows
    return pl.pallas_call(
        norm_kernel,
        out_shape=jax.ShapeDtypeStruct((rows, WIDTH), jnp.bfloat16),
        grid=(1,),
        in_specs=[pl.BlockSpec((rows, WIDTH), lambda i: (step, 0))],
        out_specs=pl.BlockSpec((rows, WIDTH), lambda i: (0, 0)),
    )(embeddings)


def lane_maxima(x):
    width = 64
    while x.shape[0] > 8:
        half = x.shape[0] // 2
        top, bottom = x[:half], x[half:]
        lane = lax.broadcasted_iota(jnp.int32, (half, 128), 1)
        low = (lane & width) == 0
        keep = jnp.where(low, top, bottom)
        give = jnp.where(low, bottom, top)
        if width == 64:
            give = pltpu.roll(give, 64, 1)
        else:
            give = jnp.where(low, pltpu.roll(give, 128 - width, 1), pltpu.roll(give, width, 1))
        x = jnp.maximum(keep, give)
        width //= 2
    return x


class Work:
    def __init__(self, data, idc, idr, seg, accr, accc):
        self.data, self.idc, self.idr, self.seg = data, idc, idr, seg
        self.accr, self.accc = accr, accc

    def span(self, slot, first, rows):
        start = self.seg[slot * 16 + first // PIECE]
        end = self.seg[slot * 16 + 8 + (first + rows) // PIECE - 1]
        return start, end

    def shares(self, a, ra, m, b, cb, n):
        a0, a1 = self.span(a, ra, m)
        b0, b1 = self.span(b, cb, n)
        return (a0 <= b1) & (b0 <= a1)

    def tile(self, a, ra, m, b, cb, n, diagonal=False):
        rows = pl.ds(pl.multiple_of(a * ROWS + ra, PIECE), m)
        cols = pl.ds(pl.multiple_of(b * ROWS + cb, PIECE), n)
        scores = lax.dot_general(
            self.data[rows, :],
            self.data[cols, :],
            (((1,), (1,)), ((), ())),
            preferred_element_type=jnp.float32,
        )
        ids = self.idc[rows, :]
        best = self.accr[rows, :]
        for g in range(n // 128):
            at = pl.ds(pl.multiple_of(cb + g * 128, 128), 128)
            same = ids == self.idr[b, :, at]
            if diagonal:
                row = lax.broadcasted_iota(jnp.int32, (m, 128), 0) + ra
                col = lax.broadcasted_iota(jnp.int32, (m, 128), 1) + (cb + g * 128)
                same = same & (row != col)
            v = jnp.where(same, scores[:, g * 128 : (g + 1) * 128], 0.0)
            best = jnp.maximum(best, v)
            self.accc[b, :, at] = jnp.maximum(
                self.accc[b, :, at], jnp.max(v.reshape(m // 8, 8, 128), axis=0)
            )
        self.accr[rows, :] = best

    def finish(self, r_ref, c_ref):
        for s in range(r_ref.shape[0]):
            r_ref[s] = lane_maxima(self.accr[s * ROWS : (s + 1) * ROWS, :])
            c_ref[s] = jnp.max(self.accc[s], axis=0, keepdims=True)


def own_kernel(core_ref, seg_ref, own_ref, sib_ref, idc_ref, idr_ref, r_ref, c_ref, data, accr, accc):
    accr[...] = jnp.zeros_like(accr)
    accc[...] = jnp.zeros_like(accc)
    data[0:ROWS, :] = own_ref[...]
    data[ROWS:, :] = sib_ref[...]
    work = Work(data, idc_ref, idr_ref, seg_ref, accr, accc)
    size = 512

    def within(i, _):
        ra, cb = lax.div(i, 2) * size, lax.rem(i, 2) * size

        @pl.when(work.shares(0, ra, size, 0, cb, size))
        def _():
            work.tile(0, ra, size, 0, cb, size, diagonal=True)

        return 0

    lax.fori_loop(0, 4, within, 0)
    core = core_ref[0]

    def between(i, _):
        ra, cb = core * size, i * size

        @pl.when(work.shares(core, ra, size, 1 - core, cb, size))
        def _():
            work.tile(core, ra, size, 1 - core, cb, size)

        return 0

    lax.fori_loop(0, 2, between, 0)
    work.finish(r_ref, c_ref)


def step_kernel(step, seg_ref, own_ref_t, other_ref_t, idc_ref, idr_ref, *refs):
    count = step + 1
    arrays = refs[: 2 + 4 * count]
    r_ref, c_ref, data, accr, accc, sems = refs[2 + 4 * count :]
    edges = [0]
    for size in CHUNKS:
        edges.append(edges[-1] + size)
    first, size = edges[step], CHUNKS[step]

    def copies():
        out = []
        for s in range(2):
            out.append(pltpu.make_async_copy(arrays[s], data.at[pl.ds(s * ROWS, ROWS)], sems.at[0]))
        for s in range(4):
            k = step
            out.append(
                pltpu.make_async_copy(
                    arrays[2 + s * count + k],
                    data.at[pl.ds((2 + s) * ROWS + edges[k], CHUNKS[k])],
                    sems.at[0],
                )
            )
        late = []
        for s in range(4):
            for k in range(step):
                late.append(
                    pltpu.make_async_copy(
                        arrays[2 + s * count + k],
                        data.at[pl.ds((2 + s) * ROWS + edges[k], CHUNKS[k])],
                        sems.at[1],
                    )
                )
        return out, late

    soon, late = copies()
    for c in soon + late:
        c.start()
    accr[...] = jnp.zeros_like(accr)
    accc[...] = jnp.zeros_like(accc)
    work = Work(data, idc_ref, idr_ref, seg_ref, accr, accc)
    for c in soon:
        c.wait()

    def own_tile(t, _):
        a, b = own_ref_t[1 + 2 * t], own_ref_t[2 + 2 * t]

        @pl.when(work.shares(a, 0, ROWS, b, first, size))
        def _():
            work.tile(a, 0, ROWS, b, first, size)

        return 0

    lax.fori_loop(0, own_ref_t[0], own_tile, 0)
    for c in late:
        c.wait()

    def other_tile(t, _):
        a, b = other_ref_t[1 + 2 * t], other_ref_t[2 + 2 * t]

        @pl.when(work.shares(a, 0, first + size, b, first, size))
        def _():
            work.tile(a, 0, first + size, b, first, size)

        if first > 0:

            @pl.when(work.shares(a, first, size, b, 0, first))
            def _():
                work.tile(a, first, size, b, 0, first)

        return 0

    lax.fori_loop(0, other_ref_t[0], other_tile, 0)
    work.finish(r_ref, c_ref)


VMEM = pl.BlockSpec(memory_space=pltpu.VMEM)
SMEM = pl.BlockSpec(memory_space=pltpu.SMEM)
HBM = pl.BlockSpec(memory_space=pl.ANY)
PARAMS = pltpu.CompilerParams(vmem_limit_bytes=56 * 2**20)


def outputs(slots):
    return (
        jax.ShapeDtypeStruct((slots, 8, 128), jnp.float32),
        jax.ShapeDtypeStruct((slots, 1, ROWS), jnp.float32),
    )


def scratch(slots):
    return [
        pltpu.VMEM((slots * ROWS, WIDTH), jnp.bfloat16),
        pltpu.VMEM((slots * ROWS, 128), jnp.float32),
        pltpu.VMEM((slots, 8, ROWS), jnp.float32),
    ]


def own_maxima(core, seg, own, sibling, idc, idr):
    return pl.pallas_call(
        own_kernel,
        out_shape=outputs(2),
        in_specs=[SMEM, SMEM, VMEM, VMEM, VMEM, VMEM],
        out_specs=(VMEM, VMEM),
        scratch_shapes=scratch(2),
        compiler_params=PARAMS,
    )(core, seg, own, sibling, idc, idr)


def step_maxima(step, seg, own_tiles, other_tiles, idc, idr, arrays):
    return pl.pallas_call(
        functools.partial(step_kernel, step),
        out_shape=outputs(SLOTS),
        in_specs=[SMEM, SMEM, SMEM, VMEM, VMEM] + [HBM] * len(arrays),
        out_specs=(VMEM, VMEM),
        scratch_shapes=scratch(SLOTS) + [pltpu.SemaphoreType.DMA((2,))],
        compiler_params=PARAMS,
    )(seg, own_tiles, other_tiles, idc, idr, *arrays)


def by_row(r, c):
    return jnp.maximum(jnp.swapaxes(r, 1, 2).reshape(r.shape[0], ROWS), c[:, 0, :])


def local(embeddings, cluster_sizes):
    count = lax.axis_size(AXIS)
    clusters = cluster_sizes.shape[0]
    me = lax.axis_index(AXIS)
    kind = lax.rem(me, RING)
    ring = me - kind

    ends = jnp.cumsum(cluster_sizes)
    blocks = (jnp.asarray(BLOCKS)[kind] + ring) % count
    pos = blocks[:, None] * ROWS + jnp.arange(ROWS, dtype=jnp.int32)[None, :]
    ids = jnp.sum((ends[None, None, :] <= pos[:, :, None]).astype(jnp.int32), axis=2)
    seg = jnp.concatenate([ids[:, ::PIECE], ids[:, PIECE - 1 :: PIECE]], axis=1).reshape(-1)
    idr = ids.astype(jnp.float32)[:, None, :]
    idc = jnp.broadcast_to(ids.astype(jnp.float32).reshape(SLOTS * ROWS, 1), (SLOTS * ROWS, 128))
    own_tiles = jnp.asarray(OWN_TILES)[kind]
    other_tiles = jnp.asarray(OTHER_TILES)[kind]

    swap = [(i, i ^ 1) for i in range(count)]
    ways = routes(count)
    parts = []
    first = 0
    for size in CHUNKS:
        parts.append(normalize(embeddings, first, size))
        first += size
    own = jnp.concatenate(parts, axis=0)
    got = [[lax.ppermute(part, AXIS, way) for way in ways] for part in parts]
    sibling = lax.ppermute(own, AXIS, swap)

    found = []
    r, c = own_maxima(
        lax.rem(me, 2).reshape(1), seg, own, sibling, idc[: 2 * ROWS], idr[:2]
    )
    base = by_row(r, c)
    for step in range(len(CHUNKS)):
        r0, r1, r2 = got[step]
        passed = jnp.where(kind == 0, r1, jnp.where(kind == 1, r2, r0))
        got[step].append(lax.ppermute(passed, AXIS, swap))
        arrays = [own, sibling] + [got[k][s] for s in range(4) for k in range(step + 1)]
        found.append(step_maxima(step, seg, own_tiles, other_tiles, idc, idr, arrays))
    r = functools.reduce(jnp.maximum, [f[0] for f in found])
    c = functools.reduce(jnp.maximum, [f[1] for f in found])
    best = by_row(r, c)
    best = jnp.concatenate([jnp.maximum(best[:2], base), best[2:]], axis=0)

    bins = jnp.arange(clusters, dtype=jnp.int32)
    peaks = jnp.max(jnp.where(ids[None] == bins[:, None, None], best[None], 0.0), axis=(1, 2))
    devices = jnp.arange(count, dtype=jnp.int32)
    to = devices[:, None] == blocks[None, :]
    rows = jnp.max(jnp.where(to[:, :, None], best[None], 0.0), axis=1)
    tail = jnp.broadcast_to(peaks[None, :], (count, clusters))
    pad = jnp.zeros((count, 128 - clusters), jnp.float32)
    sent = jnp.concatenate([rows, tail, pad], axis=1).reshape(count, 9, 128)
    back = lax.all_to_all(sent, AXIS, 0, 0, tiled=True)
    final = jnp.max(back, axis=0) * (1.0 / WIDTH)
    return final[:8].reshape(ROWS), final[8, :clusters]


def solution(mesh):
    placed = (P(AXIS, None), P())
    return jax.shard_map(
        local, mesh=mesh, in_specs=placed, out_specs=(P(AXIS), P()), check_vma=False
    )
```

time: 527 us -> 166 us (0.31)
  waiting for transfers between devices: 305 us -> 12.8 us
  blocking collectives: 102 us -> 37.1 us
  Pallas kernels: 0 us -> 59.2 us
  starting transfers between devices: 75 us -> 32.2 us
  matrix products: 37.8 us -> 0 us
  local copies, waits for them, and re-layouts: 0.11 us -> 12.1 us
  other arithmetic: 4.87 us -> 12 us
    ppermute x16 -> x17, waiting for transfers between devices: 305 us -> 12.8 us  [the longest x12 12.8 us: local(): got = [[lax.ppermute(part, AXIS, way) for way in ways] for part in parts]]
    pmax x1 -> x0, blocking collectives: 102 us -> none  [local(): cluster_max = lax.pmax(local_peaks, 'docs')]
    pallas_call x0 -> x9, Pallas kernels: none -> 59.2 us  [the longest x4 41.8 us: step_maxima(): pl.pallas_call(functools.partial(step_kernel, step), out_shape=outputs(SL...]
    ppermute x16 -> x17, starting transfers between devices: 75 us -> 32.2 us  [the longest x12 31.6 us: local(): got = [[lax.ppermute(part, AXIS, way) for way in ways] for part in parts]]
    dot_general x9 -> x0, matrix products: 37.8 us -> none  [tile_maxima(): lax.dot_general(left_block, right_block, (((1,), (1,)), ((), ())), prefer...]
    all_to_all x0 -> x1, blocking collectives: none -> 37.1 us  [local(): back = lax.all_to_all(sent, AXIS, 0, 0, tiled=True)]
    select_n x5 -> x4, other arithmetic: 0.03 us -> 5.98 us  [local(): passed = jnp.where(kind == 0, r1, jnp.where(kind == 1, r2, r0))]
  transfers between devices with their start and end apart: 16 -> 17, of which waited for: 9 -> 4; matrix products, arithmetic and copies ran while one was open for 7% -> 11% of each run, Pallas kernels for 0% -> 27%
where the time goes in v1:
time: 166 us
  Pallas kernels  59.2 us (36%)
  blocking collectives  37.1 us (22%)
  starting transfers between devices  32.2 us (19%)
  waiting for transfers between devices  12.8 us (8%)
  local copies, waits for them, and re-layouts  12.1 us (7%)
  other arithmetic  12 us (7%)
    pallas_call x4, Pallas kernels, step_maxima(): pl.pallas_call(functools.partial(step_kernel, step), out_shape=outputs(SL...  41.8 us
    all_to_all x1, blocking collectives, local(): back = lax.all_to_all(sent, AXIS, 0, 0, tiled=True)  37.1 us
    ppermute x12, starting transfers between devices, local(): got = [[lax.ppermute(part, AXIS, way) for way in ways] for part in parts]  31.6 us
    ppermute x12, waiting for transfers between devices, local(): got = [[lax.ppermute(part, AXIS, way) for way in ways] for part in parts]  12.8 us
    pallas_call x1, Pallas kernels, own_maxima(): pl.pallas_call(own_kernel, out_shape=outputs(2), in_specs=[SMEM, SMEM, VM...  9.25 us
    pallas_call x4, Pallas kernels, normalize(): pl.pallas_call(norm_kernel, out_shape=jax.ShapeDtypeStruct((rows, WIDTH),...  8.16 us
    select_n x4, other arithmetic, local(): passed = jnp.where(kind == 0, r1, jnp.where(kind == 1, r2, r0))  5.98 us
    broadcast_in_dim x2, local copies, waits for them, and re-layouts, local(): jnp.broadcast_to(ids.astype(jnp.float32).reshape(SLOTS * ROWS, 1), (SLOTS...  3.47 us
  transfers between devices with their start and end apart: 17, of which 4 were waited for; matrix products, arithmetic and copies ran while one was open for 11% of the time, Pallas kernels for 27%

profile of v1, /device:TPU:1, one launch (start us, length us, event | category | flops | bytes accessed | tf_op | source)
XLA Modules:
  0.0 166.4 jit_solution(6798823791754957940)
XLA Ops:
  0.6 2.0 %shard_map.70 = bf16[256,1024]{1,0:T(8,128)(2,1)} custom-call(bf16[1024,1024]{1,0:T(8,128)(2,1)} %x_ref.7), custom_call_target="tpu_custom_call" | custom-call | tf_op jit(solution)/shard_map/pallas_call | solution.py:117
  2.7 3.0 %collective-permute-start.11 = (bf16[256,1024]{1,0:T(8,128)(2,1)}, bf16[256,1024]{1,0:T(8,128)(2,1)S(1)}, u32[]{:S(2)}, u32[]{:S(2)}) collective-permute-start(bf16[256,1024]{1,0:T(8,128)(2,1)} %shard_map.70), channel_id=1, source_target_pairs={{8,0},{7,1},{1,2},{123,3},{13,4},{10,5},{4,6},{14,7},{16,8},{15,9}... | collective-permute-start | bytes 1572872 | tf_op jit(solution)/shard_map/ppermute | solution.py:370
  5.7 4.9 %collective-permute-start.10 = (bf16[256,1024]{1,0:T(8,128)(2,1)}, bf16[256,1024]{1,0:T(8,128)(2,1)S(1)}, u32[]{:S(2)}, u32[]{:S(2)}) collective-permute-start(bf16[256,1024]{1,0:T(8,128)(2,1)} %shard_map.70), channel_id=1, source_target_pairs={{6,0},{9,1},{122,2},{0,3},{11,4},{12,5},{125,6},{127,7},{14,8},{17... | collective-permute-start | bytes 1572872 | tf_op jit(solution)/shard_map/ppermute | solution.py:370
  10.6 2.0 %shard_map.71 = bf16[256,1024]{1,0:T(8,128)(2,1)} custom-call(bf16[1024,1024]{1,0:T(8,128)(2,1)} %x_ref.7), custom_call_target="tpu_custom_call" | custom-call | tf_op jit(solution)/shard_map/pallas_call | solution.py:117
  13.7 5.1 %collective-permute-start.14 = (bf16[256,1024]{1,0:T(8,128)(2,1)}, bf16[256,1024]{1,0:T(8,128)(2,1)}, u32[]{:S(2)}, u32[]{:S(2)}) collective-permute-start(bf16[256,1024]{1,0:T(8,128)(2,1)} %shard_map.71), channel_id=1, source_target_pairs={{6,0},{9,1},{122,2},{0,3},{11,4},{12,5},{125,6},{127,7},{14,8},{17... | collective-permute-start | bytes 1572872 | tf_op jit(solution)/shard_map/ppermute | solution.py:370
  18.8 2.1 %shard_map.69 = bf16[256,1024]{1,0:T(8,128)(2,1)} custom-call(bf16[1024,1024]{1,0:T(8,128)(2,1)} %x_ref.7), custom_call_target="tpu_custom_call" | custom-call | tf_op jit(solution)/shard_map/pallas_call | solution.py:117
  20.9 2.0 %shard_map.68 = bf16[256,1024]{1,0:T(8,128)(2,1)} custom-call(bf16[1024,1024]{1,0:T(8,128)(2,1)} %x_ref.7), custom_call_target="tpu_custom_call" | custom-call | tf_op jit(solution)/shard_map/pallas_call | solution.py:117
  26.3 2.1 %collective-permute-start.13 = (bf16[256,1024]{1,0:T(8,128)(2,1)}, bf16[256,1024]{1,0:T(8,128)(2,1)}, u32[]{:S(2)}, u32[]{:S(2)}) collective-permute-start(bf16[256,1024]{1,0:T(8,128)(2,1)} %shard_map.71), channel_id=1, source_target_pairs={{2,0},{3,1},{5,2},{124,3},{6,4},{7,5},{0,6},{1,7},{10,8},{11,9},{1... | collective-permute-start | bytes 1572872 | tf_op jit(solution)/shard_map/ppermute | solution.py:370
  29.6 5.4 %collective-permute-start.2 = (bf16[256,1024]{1,0:T(8,128)(2,1)}, bf16[256,1024]{1,0:T(8,128)(2,1)S(1)}, u32[]{:S(2)}, u32[]{:S(2)}) collective-permute-start(bf16[256,1024]{1,0:T(8,128)(2,1)} %shard_map.68), channel_id=1, source_target_pairs={{6,0},{9,1},{122,2},{0,3},{11,4},{12,5},{125,6},{127,7},{14,8},{17... | collective-permute-start | bytes 1572872 | tf_op jit(solution)/shard_map/ppermute | solution.py:370
  37.0 1.9 %select_select_fusion.1 = bf16[256,1024]{1,0:T(8,128)(2,1)} fusion(bf16[256,1024]{1,0:T(8,128)(2,1)} %copy-done.9, bf16[256,1024]{1,0:T(8,128)(2,1)} %copy-done.8, bf16[256,1024]{1,0:T(8,128)(2,1)} %collective-permute-done.9.refs_4_, pred[]{:T(512)S(6)} %eq.51, pred[]{:T(512)S(6)} %eq.50), kind=kLoop, calls=%fused_computation.6 | loop fusion | flops 524288 | bytes 2097154 | tf_op jit(solution)/shard_map/jit(_where)/select_n | solution.py:380
  38.9 2.4 %collective-permute-done.13.refs_5_ = bf16[256,1024]{1,0:T(8,128)(2,1)} collective-permute-done((bf16[256,1024]{1,0:T(8,128)(2,1)}, bf16[256,1024]{1,0:T(8,128)(2,1)}, u32[]{:S(2)}, u32[]{:S(2)}) %collective-permute-start.13) | collective-permute-done | bytes 524320 | tf_op jit(solution)/shard_map/ppermute | solution.py:370
  41.3 2.8 %collective-permute-start.7 = (bf16[256,1024]{1,0:T(8,128)(2,1)S(1)}, bf16[256,1024]{1,0:T(8,128)(2,1)S(1)}, u32[]{:S(2)}, u32[]{:S(2)}) collective-permute-start(bf16[256,1024]{1,0:T(8,128)(2,1)S(1)} %copy-done.11), channel_id=1, source_target_pairs={{8,0},{7,1},{1,2},{123,3},{13,4},{10,5},{4,6},{14,7},{16,8},{15,9}... | collective-permute-start | bytes 1572872 | tf_op jit(solution)/shard_map/ppermute | solution.py:370
  44.2 5.9 %collective-permute-start.6 = (bf16[256,1024]{1,0:T(8,128)(2,1)S(1)}, bf16[256,1024]{1,0:T(8,128)(2,1)S(1)}, u32[]{:S(2)}, u32[]{:S(2)}) collective-permute-start(bf16[256,1024]{1,0:T(8,128)(2,1)S(1)} %copy-done.11), channel_id=1, source_target_pairs={{6,0},{9,1},{122,2},{0,3},{11,4},{12,5},{125,6},{127,7},{14,8},{17... | collective-permute-start | bytes 1572872 | tf_op jit(solution)/shard_map/ppermute | solution.py:370
  50.1 2.1 %select_select_fusion = bf16[256,1024]{1,0:T(8,128)(2,1)} fusion(bf16[256,1024]{1,0:T(8,128)(2,1)} %collective-permute-done.14.refs_9_, bf16[256,1024]{1,0:T(8,128)(2,1)} %collective-permute-done.15.refs_13_, bf16[256,1024]{1,0:T(8,128)(2,1)} %collective-permute-done.13.refs_5_, pred[]{:T(512)S(6)} %eq.51, pred[]{:T(512)S(6)} %eq.50), kind=kLoop, calls=%fused_computation.5 | loop fusion | flops 524288 | bytes 2097154 | tf_op jit(solution)/shard_map/jit(_where)/select_n | solution.py:380
  52.2 2.1 %collective-permute-done.1.refs_2_ = bf16[256,1024]{1,0:T(8,128)(2,1)S(1)} collective-permute-done((bf16[256,1024]{1,0:T(8,128)(2,1)}, bf16[256,1024]{1,0:T(8,128)(2,1)S(1)}, u32[]{:S(2)}, u32[]{:S(2)}) %collective-permute-start.1) | collective-permute-done | bytes 524320 | tf_op jit(solution)/shard_map/ppermute | solution.py:370
  55.8 2.8 %collective-permute-done.6.refs_5_.refs_6_.refs_7_ = bf16[256,1024]{1,0:T(8,128)(2,1)S(1)} collective-permute-done((bf16[256,1024]{1,0:T(8,128)(2,1)S(1)}, bf16[256,1024]{1,0:T(8,128)(2,1)S(1)}, u32[]{:S(2)}, u32[]{:S(2)}) %collective-permute-start.6) | collective-permute-done | bytes 524320 | tf_op jit(solution)/shard_map/ppermute | solution.py:370
  58.6 5.4 %collective-permute-done.5.refs_3_ = bf16[256,1024]{1,0:T(8,128)(2,1)S(1)} collective-permute-done((bf16[256,1024]{1,0:T(8,128)(2,1)S(1)}, bf16[256,1024]{1,0:T(8,128)(2,1)S(1)}, u32[]{:S(2)}, u32[]{:S(2)}) %collective-permute-start.5) | collective-permute-done | bytes 524320 | tf_op jit(solution)/shard_map/ppermute | solution.py:370
  69.5 9.3 %shard_map.76 = (f32[2,8,128]{2,1,0:T(8,128)}, f32[2,1,1024]{2,1,0:T(1,128)}) custom-call(s32[1]{0:T(128)} %bitcast.8.core_ref, s32[96]{0:T(128)} %reshape.137.seg_ref, bf16[1024,1024]{1,0:T(8,128)(2,1)} %copy-done, bf16[1024,1024]{1,0:T(8,128)(2,1)} %collective-permute-done.refs_1_.sib_ref, f32[2048,128]{1,0:T(8,128)} %broadcast_in_dim.62.idc_ref, ...), custom_call_target="tpu_custom_call" | custom-call | tf_op jit(solution)/shard_map/pallas_call | solution.py:320
  79.8 2.1 %broadcast_in_dim.41.idc_ref = f32[6144,128]{1,0:T(8,128)} broadcast(f32[6144]{0:T(1024)S(1)} %convert_element_type.31), dimensions={0} | broadcast | bytes 3170304 | tf_op jit(solution)/shard_map/broadcast_in_dim | solution.py:358
  81.9 8.8 %shard_map.72 = (f32[6,8,128]{2,1,0:T(8,128)}, f32[6,1,1024]{2,1,0:T(1,128)}) custom-call(s32[96]{0:T(128)} %reshape.137.seg_ref, s32[9]{0:T(128)} %fusion.1.own_ref_t, s32[11]{0:T(128)} %fusion.2.other_ref_t, f32[6144,128]{1,0:T(8,128)} %broadcast_in_dim.41.idc_ref, f32[6,1,1024]{2,1,0:T(1,128)} %copy.42.idr_ref, bf16[1024,1024]{1,0:T(8,128)(2,1)} %copy-done, ...), custom_call_target="tpu_custom_call" | custom-call | tf_op jit(solution)/shard_map/pallas_call | solution.py:331
  91.5 10.0 %shard_map.73 = (f32[6,8,128]{2,1,0:T(8,128)}, f32[6,1,1024]{2,1,0:T(1,128)}) custom-call(s32[96]{0:T(128)} %reshape.137.seg_ref, s32[9]{0:T(128)} %fusion.1.own_ref_t, s32[11]{0:T(128)} %fusion.2.other_ref_t, f32[6144,128]{1,0:T(8,128)} %broadcast_in_dim.41.idc_ref, f32[6,1,1024]{2,1,0:T(1,128)} %copy.42.idr_ref, bf16[1024,1024]{1,0:T(8,128)(2,1)} %copy-done, ...), custom_call_target="tpu_custom_call" | custom-call | tf_op jit(solution)/shard_map/pallas_call | solution.py:331
  101.5 11.0 %shard_map.74 = (f32[6,8,128]{2,1,0:T(8,128)}, f32[6,1,1024]{2,1,0:T(1,128)}) custom-call(s32[96]{0:T(128)} %reshape.137.seg_ref, s32[9]{0:T(128)} %fusion.1.own_ref_t, s32[11]{0:T(128)} %fusion.2.other_ref_t, f32[6144,128]{1,0:T(8,128)} %broadcast_in_dim.41.idc_ref, f32[6,1,1024]{2,1,0:T(1,128)} %copy.42.idr_ref, bf16[1024,1024]{1,0:T(8,128)(2,1)} %copy-done, ...), custom_call_target="tpu_custom_call" | custom-call | tf_op jit(solution)/shard_map/pallas_call | solution.py:331
  112.6 12.0 %shard_map.75 = (f32[6,8,128]{2,1,0:T(8,128)}, f32[6,1,1024]{2,1,0:T(1,128)}) custom-call(s32[96]{0:T(128)} %reshape.137.seg_ref, s32[9]{0:T(128)} %fusion.1.own_ref_t, s32[11]{0:T(128)} %fusion.2.other_ref_t, f32[6144,128]{1,0:T(8,128)} %broadcast_in_dim.41.idc_ref, f32[6,1,1024]{2,1,0:T(1,128)} %copy.42.idr_ref, bf16[1024,1024]{1,0:T(8,128)(2,1)} %copy-done, ...), custom_call_target="tpu_custom_call" | custom-call | tf_op jit(solution)/shard_map/pallas_call | solution.py:331
  128.0 37.1 %all_to_all.5 = f32[128,9,128]{2,1,0:T(8,128)S(1)} all-to-all(f32[128,9,128]{2,1,0:T(8,128)S(1)} %copy.53), channel_id=1, replica_groups=mesh['docs'=128] {'docs'}, dimensions={0} | all-to-all | bytes 1179648 | tf_op jit(solution)/shard_map/all_to_all | solution.py:397
  (107 shorter events, 20.9 us)
Async XLA Ops:
  2.7 23.3 %collective-permute-start.11 = (bf16[256,1024]{1,0:T(8,128)(2,1)}, bf16[256,1024]{1,0:T(8,128)(2,1)S(1)}, u32[]{:S(2)}, u32[]{:S(2)}) collective-permute-start(bf16[256,1024]{1,0:T(8,128)(2,1)} %shard_map.70), channel_id=1, source_target_pairs={{8,0},{7,1},{1,2},{123,3},{13,4},{10,5},{4,6},{14,7},{16,8},{15,9}... | collective-permute-start | bytes 1572872 | tf_op jit(solution)/shard_map/ppermute | solution.py:370
  5.7 20.6 %collective-permute-start.10 = (bf16[256,1024]{1,0:T(8,128)(2,1)}, bf16[256,1024]{1,0:T(8,128)(2,1)S(1)}, u32[]{:S(2)}, u32[]{:S(2)}) collective-permute-start(bf16[256,1024]{1,0:T(8,128)(2,1)} %shard_map.70), channel_id=1, source_target_pairs={{6,0},{9,1},{122,2},{0,3},{11,4},{12,5},{125,6},{127,7},{14,8},{17... | collective-permute-start | bytes 1572872 | tf_op jit(solution)/shard_map/ppermute | solution.py:370
  10.6 17.8 %collective-permute-start.9 = (bf16[256,1024]{1,0:T(8,128)(2,1)}, bf16[256,1024]{1,0:T(8,128)(2,1)}, u32[]{:S(2)}, u32[]{:S(2)}) collective-permute-start(bf16[256,1024]{1,0:T(8,128)(2,1)} %shard_map.70), channel_id=1, source_target_pairs={{2,0},{3,1},{5,2},{124,3},{6,4},{7,5},{0,6},{1,7},{10,8},{11,9},{1... | collective-permute-start | bytes 1572872 | tf_op jit(solution)/shard_map/ppermute | solution.py:370
  12.7 17.0 %collective-permute-start.15 = (bf16[256,1024]{1,0:T(8,128)(2,1)}, bf16[256,1024]{1,0:T(8,128)(2,1)}, u32[]{:S(2)}, u32[]{:S(2)}) collective-permute-start(bf16[256,1024]{1,0:T(8,128)(2,1)} %shard_map.71), channel_id=1, source_target_pairs={{8,0},{7,1},{1,2},{123,3},{13,4},{10,5},{4,6},{14,7},{16,8},{15,9}... | collective-permute-start | bytes 1572872 | tf_op jit(solution)/shard_map/ppermute | solution.py:370
  13.7 23.2 %collective-permute-start.14 = (bf16[256,1024]{1,0:T(8,128)(2,1)}, bf16[256,1024]{1,0:T(8,128)(2,1)}, u32[]{:S(2)}, u32[]{:S(2)}) collective-permute-start(bf16[256,1024]{1,0:T(8,128)(2,1)} %shard_map.71), channel_id=1, source_target_pairs={{6,0},{9,1},{122,2},{0,3},{11,4},{12,5},{125,6},{127,7},{14,8},{17... | collective-permute-start | bytes 1572872 | tf_op jit(solution)/shard_map/ppermute | solution.py:370
  25.9 26.2 %copy-start = (bf16[1024,1024]{1,0:T(8,128)(2,1)}, bf16[1024,1024]{1,0:T(8,128)(2,1)S(1)}, u32[]{:S(2)}) copy-start(bf16[1024,1024]{1,0:T(8,128)(2,1)S(1)} %pad_maximum_fusion.refs_0_.own_ref) | copy-start | bytes 6291460
  26.0 42.2 %collective-permute-start = (bf16[1024,1024]{1,0:T(8,128)(2,1)S(1)}, bf16[1024,1024]{1,0:T(8,128)(2,1)}, u32[]{:S(2)}, u32[]{:S(2)}) collective-permute-start(bf16[1024,1024]{1,0:T(8,128)(2,1)S(1)} %pad_maximum_fusion.refs_0_.own_ref), channel_id=1, source_target_pairs={{0,1},{1,0},{2,3},{3,2},{4,5},{5,4},{6,7},{7,6},{8,9},{9,8},{10,11... | collective-permute-start | bytes 6291464 | tf_op jit(solution)/shard_map/ppermute | solution.py:371
  26.3 15.1 %collective-permute-start.13 = (bf16[256,1024]{1,0:T(8,128)(2,1)}, bf16[256,1024]{1,0:T(8,128)(2,1)}, u32[]{:S(2)}, u32[]{:S(2)}) collective-permute-start(bf16[256,1024]{1,0:T(8,128)(2,1)} %shard_map.71), channel_id=1, source_target_pairs={{2,0},{3,1},{5,2},{124,3},{6,4},{7,5},{0,6},{1,7},{10,8},{11,9},{1... | collective-permute-start | bytes 1572872 | tf_op jit(solution)/shard_map/ppermute | solution.py:370
  28.4 15.8 %collective-permute-start.3 = (bf16[256,1024]{1,0:T(8,128)(2,1)}, bf16[256,1024]{1,0:T(8,128)(2,1)S(1)}, u32[]{:S(2)}, u32[]{:S(2)}) collective-permute-start(bf16[256,1024]{1,0:T(8,128)(2,1)} %shard_map.68), channel_id=1, source_target_pairs={{8,0},{7,1},{1,2},{123,3},{13,4},{10,5},{4,6},{14,7},{16,8},{15,9}... | collective-permute-start | bytes 1572872 | tf_op jit(solution)/shard_map/ppermute | solution.py:370
  29.6 20.4 %collective-permute-start.2 = (bf16[256,1024]{1,0:T(8,128)(2,1)}, bf16[256,1024]{1,0:T(8,128)(2,1)S(1)}, u32[]{:S(2)}, u32[]{:S(2)}) collective-permute-start(bf16[256,1024]{1,0:T(8,128)(2,1)} %shard_map.68), channel_id=1, source_target_pairs={{6,0},{9,1},{122,2},{0,3},{11,4},{12,5},{125,6},{127,7},{14,8},{17... | collective-permute-start | bytes 1572872 | tf_op jit(solution)/shard_map/ppermute | solution.py:370
  37.0 17.3 %collective-permute-start.1 = (bf16[256,1024]{1,0:T(8,128)(2,1)}, bf16[256,1024]{1,0:T(8,128)(2,1)S(1)}, u32[]{:S(2)}, u32[]{:S(2)}) collective-permute-start(bf16[256,1024]{1,0:T(8,128)(2,1)} %shard_map.68), channel_id=1, source_target_pairs={{2,0},{3,1},{5,2},{124,3},{6,4},{7,5},{0,6},{1,7},{10,8},{11,9},{1... | collective-permute-start | bytes 1572872 | tf_op jit(solution)/shard_map/ppermute | solution.py:370
  41.3 13.9 %collective-permute-start.7 = (bf16[256,1024]{1,0:T(8,128)(2,1)S(1)}, bf16[256,1024]{1,0:T(8,128)(2,1)S(1)}, u32[]{:S(2)}, u32[]{:S(2)}) collective-permute-start(bf16[256,1024]{1,0:T(8,128)(2,1)S(1)} %copy-done.11), channel_id=1, source_target_pairs={{8,0},{7,1},{1,2},{123,3},{13,4},{10,5},{4,6},{14,7},{16,8},{15,9}... | collective-permute-start | bytes 1572872 | tf_op jit(solution)/shard_map/ppermute | solution.py:370
  44.2 14.4 %collective-permute-start.6 = (bf16[256,1024]{1,0:T(8,128)(2,1)S(1)}, bf16[256,1024]{1,0:T(8,128)(2,1)S(1)}, u32[]{:S(2)}, u32[]{:S(2)}) collective-permute-start(bf16[256,1024]{1,0:T(8,128)(2,1)S(1)} %copy-done.11), channel_id=1, source_target_pairs={{6,0},{9,1},{122,2},{0,3},{11,4},{12,5},{125,6},{127,7},{14,8},{17... | collective-permute-start | bytes 1572872 | tf_op jit(solution)/shard_map/ppermute | solution.py:370
  50.1 14.0 %collective-permute-start.5 = (bf16[256,1024]{1,0:T(8,128)(2,1)S(1)}, bf16[256,1024]{1,0:T(8,128)(2,1)S(1)}, u32[]{:S(2)}, u32[]{:S(2)}) collective-permute-start(bf16[256,1024]{1,0:T(8,128)(2,1)S(1)} %copy-done.11), channel_id=1, source_target_pairs={{2,0},{3,1},{5,2},{124,3},{6,4},{7,5},{0,6},{1,7},{10,8},{11,9},{1... | collective-permute-start | bytes 1572872 | tf_op jit(solution)/shard_map/ppermute | solution.py:370
  54.3 47.2 %collective-permute-start.12 = (bf16[256,1024]{1,0:T(8,128)(2,1)}, bf16[256,1024]{1,0:T(8,128)(2,1)}, u32[]{:S(2)}, u32[]{:S(2)}) collective-permute-start(bf16[256,1024]{1,0:T(8,128)(2,1)} %select_select_fusion.1), channel_id=1, source_target_pairs={{0,1},{1,0},{2,3},{3,2},{4,5},{5,4},{6,7},{7,6},{8,9},{9,8},{10,11... | collective-permute-start | bytes 1572872 | tf_op jit(solution)/shard_map/ppermute | solution.py:381
  55.3 12.9 %copy-start.5 = (bf16[256,1024]{1,0:T(8,128)(2,1)}, bf16[256,1024]{1,0:T(8,128)(2,1)S(1)}, u32[]{:S(2)}) copy-start(bf16[256,1024]{1,0:T(8,128)(2,1)S(1)} %collective-permute-done.7.refs_7_.refs_9_.refs_11_) | copy-start | bytes 1572868
  55.3 57.3 %collective-permute-start.16 = (bf16[256,1024]{1,0:T(8,128)(2,1)}, bf16[256,1024]{1,0:T(8,128)(2,1)}, u32[]{:S(2)}, u32[]{:S(2)}) collective-permute-start(bf16[256,1024]{1,0:T(8,128)(2,1)} %select_select_fusion), channel_id=1, source_target_pairs={{0,1},{1,0},{2,3},{3,2},{4,5},{5,4},{6,7},{7,6},{8,9},{9,8},{10,11... | collective-permute-start | bytes 1572872 | tf_op jit(solution)/shard_map/ppermute | solution.py:381
  58.6 21.2 %collective-permute-start.4 = (bf16[256,1024]{1,0:T(8,128)(2,1)}, bf16[256,1024]{1,0:T(8,128)(2,1)S(1)}, u32[]{:S(2)}, u32[]{:S(2)}) collective-permute-start(bf16[256,1024]{1,0:T(8,128)(2,1)} %select_select_fusion.3), channel_id=1, source_target_pairs={{0,1},{1,0},{2,3},{3,2},{4,5},{5,4},{6,7},{7,6},{8,9},{9,8},{10,11... | collective-permute-start | bytes 1572872 | tf_op jit(solution)/shard_map/ppermute | solution.py:381
  65.0 25.7 %collective-permute-start.8 = (bf16[256,1024]{1,0:T(8,128)(2,1)}, bf16[256,1024]{1,0:T(8,128)(2,1)S(1)}, u32[]{:S(2)}, u32[]{:S(2)}) collective-permute-start(bf16[256,1024]{1,0:T(8,128)(2,1)} %select_select_fusion.2), channel_id=1, source_target_pairs={{0,1},{1,0},{2,3},{3,2},{4,5},{5,4},{6,7},{7,6},{8,9},{9,8},{10,11... | collective-permute-start | bytes 1572872 | tf_op jit(solution)/shard_map/ppermute | solution.py:381
  112.5 12.1 %copy-start.15 = (f32[6,8,128]{2,1,0:T(8,128)S(1)}, f32[6,8,128]{2,1,0:T(8,128)}, u32[]{:S(2)}) copy-start(f32[6,8,128]{2,1,0:T(8,128)} %get-tuple-element.12) | copy-start | bytes 73732
  112.5 13.2 %copy-start.12 = (f32[6,1,1024]{2,1,0:T(1,128)S(1)}, f32[6,1,1024]{2,1,0:T(1,128)}, u32[]{:S(2)}) copy-start(f32[6,1,1024]{2,1,0:T(1,128)} %get-tuple-element.16) | copy-start | bytes 73732
  112.5 13.2 %copy-start.13 = (f32[6,1,1024]{2,1,0:T(1,128)S(1)}, f32[6,1,1024]{2,1,0:T(1,128)}, u32[]{:S(2)}) copy-start(f32[6,1,1024]{2,1,0:T(1,128)} %get-tuple-element.17) | copy-start | bytes 73732
  112.5 13.2 %copy-start.14 = (f32[6,1,1024]{2,1,0:T(1,128)S(1)}, f32[6,1,1024]{2,1,0:T(1,128)}, u32[]{:S(2)}) copy-start(f32[6,1,1024]{2,1,0:T(1,128)} %get-tuple-element.18) | copy-start | bytes 73732
  112.6 14.0 %copy-start.18 = (f32[2,1,1024]{2,1,0:T(1,128)S(1)}, f32[2,1,1024]{2,1,0:T(1,128)}, u32[]{:S(2)}) copy-start(f32[2,1,1024]{2,1,0:T(1,128)} %get-tuple-element.21) | copy-start | bytes 24580
  (13 other events, 82.8 us)

commit v2 on v0

v2 whole, which is shorter than its diff:
```python
import functools

import jax
import jax.numpy as jnp
import numpy as np
from jax import lax
from jax.experimental import pallas as pl
from jax.experimental.pallas import tpu as pltpu
from jax.sharding import PartitionSpec as P

AXIS = "docs"
ROWS = 1024
WIDTH = 1024
RING = 8
SLOTS = 6
PIECE = 128
STRIP = 256
CHUNKS = (512, 512)
EDGES = (0, 512, 1024)

RECEIVED = (
    (3, 6, 9),
    (2, 8, 7),
    (-4, 1, -6),
    (5, -5, 0),
    (6, 10, 11),
    (7, 12, 13),
    (0, -1, 14),
    (1, -3, 4),
)
PASSED = (1, 2, 0, 0, 0, 0, 0, 2)
TILES = (
    ((0, 3), (0, 7), (1, 9), (3, 6), (3, 7), (3, 9), (6, 9), (7, 9)),
    ((0, 8), (1, 8), (2, 6), (2, 7), (2, 8), (6, 8)),
    ((-6, -4), (-6, 1), (-6, 2), (-4, 1), (-4, 2), (-4, 3), (1, 2), (1, 3), (1, 5)),
    ((-5, -4), (-5, 0), (-5, 2), (-5, 3), (-4, 0), (0, 2), (0, 5), (2, 5), (3, 5)),
    ((5, 10), (5, 11), (6, 10), (6, 11), (7, 10), (7, 11)),
    ((4, 6), (4, 12), (5, 6), (5, 7), (5, 13), (6, 12), (6, 13), (7, 13)),
    ((-1, 0), (-1, 4), (-1, 6), (-1, 7), (0, 4), (4, 7), (6, 14)),
    ((-3, 0), (-3, 1), (-3, 4), (0, 6), (1, 4), (1, 6), (1, 7)),
)


def slot_blocks(kind):
    sibling = kind ^ 1
    return (
        (kind, sibling) + RECEIVED[kind] + (RECEIVED[sibling][PASSED[sibling]],)
    )


def tables():
    blocks = np.array([slot_blocks(k) for k in range(RING)], np.int32)
    tiles = np.zeros((RING, 3 + 2 * max(len(v) for v in TILES)), np.int32)
    for k in range(RING):
        held = slot_blocks(k)
        pairs = sorted(tuple(sorted(held.index(v) for v in pair)) for pair in TILES[k])
        assert (0, 1) not in pairs
        tiles[k, :3] = [sum(a < e for a, _ in pairs) for e in (1, 2, SLOTS)]
        tiles[k, 3 : 3 + 2 * len(pairs)] = np.array(pairs).reshape(-1)
    return blocks, tiles


BLOCKS, KIND_TILES = tables()


def check_cover():
    seen = set()
    for k in range(RING):
        for a, b in TILES[k]:
            d = abs(a - b)
            assert d <= RING and {a, b} <= set(slot_blocks(k))
            low = min(a, b) % RING
            assert (low, d) not in seen
            seen.add((low, d))
    for low in range(RING):
        for d in range(1, RING + 1):
            assert ((low, d) in seen) != (d == 1 and low % 2 == 0)


check_cover()


def routes(count):
    out = []
    for slot in range(3):
        route = []
        for i in range(count):
            source = i - i % RING + RECEIVED[i % RING][slot]
            route.append((source % count, i))
        out.append(route)
    return out


def unit_rows(v):
    v = v.astype(jnp.float32)
    mean = jnp.sum(v * v, axis=1, keepdims=True) * (1.0 / WIDTH)
    return (v * lax.rsqrt(mean + 1e-06)).astype(jnp.bfloat16)


def norm_all_kernel(x_ref, own_ref, *part_refs):
    i = pl.program_id(0)
    normed = unit_rows(x_ref[...])
    own_ref[...] = normed
    for k, ref in enumerate(part_refs):
        lo, hi = EDGES[k + 1] // STRIP, EDGES[k + 2] // STRIP

        @pl.when((i >= lo) & (i < hi))
        def _(ref=ref):
            ref[...] = normed


def normalize_all(embeddings):
    def part_map(k):
        lo, hi = EDGES[k] // STRIP, EDGES[k + 1] // STRIP
        return lambda i: (jnp.clip(i - lo, 0, hi - lo - 1), 0)

    block = (STRIP, WIDTH)
    later = range(1, len(CHUNKS))
    return pl.pallas_call(
        norm_all_kernel,
        out_shape=[jax.ShapeDtypeStruct((ROWS, WIDTH), jnp.bfloat16)]
        + [jax.ShapeDtypeStruct((CHUNKS[k], WIDTH), jnp.bfloat16) for k in later],
        grid=(ROWS // STRIP,),
        in_specs=[pl.BlockSpec(block, lambda i: (i, 0))],
        out_specs=[pl.BlockSpec(block, lambda i: (i, 0))]
        + [pl.BlockSpec(block, part_map(k)) for k in later],
    )(embeddings)


class Work:
    def __init__(self, info, idr, idc, accr, accc):
        self.info, self.idr, self.idc = info, idr, idc
        self.accr, self.accc = accr, accc
        accr[...] = jnp.zeros_like(accr)
        accc[...] = jnp.zeros_like(accc)
        for s in range(idc.shape[0] // ROWS):
            idc[s * ROWS : (s + 1) * ROWS, :] = jnp.broadcast_to(idr[s], (128, ROWS)).T

    def span(self, slot, first, rows):
        start = self.info[slot * 16 + first // PIECE]
        end = self.info[slot * 16 + 8 + (first + rows) // PIECE - 1]
        return start, end

    def shares(self, a, ra, m, b, cb, n):
        a0, a1 = self.span(a, ra, m)
        b0, b1 = self.span(b, cb, n)
        return (a0 <= b1) & (b0 <= a1)

    def tile(self, left, a, ra, right, b, cb, diagonal=False):
        m, n = left.shape[0], right.shape[0]
        rows = pl.ds(pl.multiple_of(a * ROWS + ra, PIECE), m)
        scores = lax.dot_general(
            left, right, (((1,), (1,)), ((), ())), preferred_element_type=jnp.float32
        )
        ids = self.idc[rows, :]
        best = self.accr[rows, :]
        for g in range(n // 128):
            at = pl.ds(pl.multiple_of(cb + g * 128, 128), 128)
            same = ids == self.idr[b, :, at]
            if diagonal:
                row = lax.broadcasted_iota(jnp.int32, (m, 128), 0) + ra
                col = lax.broadcasted_iota(jnp.int32, (m, 128), 1) + (cb + g * 128)
                same = same & (row != col)
            v = jnp.where(same, scores[:, g * 128 : (g + 1) * 128], 0.0)
            best = jnp.maximum(best, v)
            self.accc[b, :, at] = jnp.maximum(
                self.accc[b, :, at], jnp.max(v.reshape(m // 8, 8, 128), axis=0)
            )
        self.accr[rows, :] = best

    def finish(self, slot, out):
        lanes = self.accr[slot * ROWS : (slot + 1) * ROWS, :]
        best = jnp.max(lanes.T.reshape(128, 8, 128), axis=0)
        cols = jnp.max(self.accc[slot], axis=0, keepdims=True)
        for v in range(8):
            out[slot, v : v + 1, :] = jnp.maximum(
                best[v : v + 1], cols[:, v * 128 : (v + 1) * 128]
            )


def own_kernel(info_ref, own_ref, idr_ref, out_ref, idc, accr, accc):
    work = Work(info_ref, idr_ref, idc, accr, accc)
    size = 512

    def within(i, _):
        ra, cb = lax.div(i, 2) * size, lax.rem(i, 2) * size

        @pl.when(work.shares(0, ra, size, 0, cb, size))
        def _():
            left = own_ref[pl.ds(pl.multiple_of(ra, size), size), :]
            right = own_ref[pl.ds(pl.multiple_of(cb, size), size), :]
            work.tile(left, 0, ra, right, 0, cb, diagonal=True)

        return 0

    lax.fori_loop(0, 4, within, 0)
    work.finish(0, out_ref)


def step_kernel(step, clusters, info_ref, idr_ref, own_ref, sib_ref, *refs):
    last = step == len(CHUNKS) - 1
    new, old, refs = refs[:4], refs[4 : 4 + 4 * step], refs[4 + 4 * step :]
    if last:
        idn_ref, earlier, refs = refs[0], refs[1 : 2 + step], refs[2 + step :]
    out_ref, idc, accr, accc, data, sems = refs[:6]
    found = refs[6] if last else out_ref
    first, size = EDGES[step], CHUNKS[step]
    copies = [
        pltpu.make_async_copy(
            old[s * step + k],
            data.at[pl.ds(s * ROWS + EDGES[k], CHUNKS[k])],
            sems.at[0],
        )
        for s in range(4)
        for k in range(step)
    ]
    for c in copies:
        c.start()
    for s in range(4):
        at = s * ROWS + first
        data[at : at + size, :] = new[s][...]
    work = Work(info_ref, idr_ref, idc, accr, accc)
    table = 16 * SLOTS + SLOTS

    def rows(slot, start, length):
        return data[pl.ds(pl.multiple_of((slot - 2) * ROWS + start, PIECE), length), :]

    def pair(t):
        return info_ref[table + 3 + 2 * t], info_ref[table + 4 + 2 * t]

    def own_tiles(ref, a):
        def body(t, _):
            b = pair(t)[1]

            @pl.when(work.shares(a, 0, ROWS, b, first, size))
            def _():
                work.tile(ref[...], a, 0, rows(b, first, size), b, first)

            return 0

        return body

    def other_tile(t, _):
        a, b = pair(t)
        end = first + size

        @pl.when(work.shares(a, 0, end, b, first, size))
        def _():
            work.tile(rows(a, 0, end), a, 0, rows(b, first, size), b, first)

        if first > 0:

            @pl.when(work.shares(a, first, size, b, 0, first))
            def _():
                work.tile(rows(a, first, size), a, first, rows(b, 0, first), b, 0)

        return 0

    ends = [info_ref[table + i] for i in range(3)]
    lax.fori_loop(0, ends[0], own_tiles(own_ref, 0), 0)
    lax.fori_loop(ends[0], ends[1], own_tiles(sib_ref, 1), 0)
    if step == 0:
        half = ROWS // 2
        core = lax.rem(info_ref[16 * SLOTS], 2)
        for c, (left, right) in enumerate(((own_ref, sib_ref), (sib_ref, own_ref))):

            @pl.when((core == c) & work.shares(c, c * half, half, 1 - c, 0, ROWS))
            def _(c=c, left=left, right=right):
                work.tile(left[c * half : (c + 1) * half, :], c, c * half, right[...], 1 - c, 0)

    for c in copies:
        c.wait()
    lax.fori_loop(ends[1], ends[2], other_tile, 0)
    for s in range(SLOTS):
        work.finish(s, found)
    if not last:
        return

    for s in range(SLOTS):
        best = found[s]
        for ref in earlier[1:]:
            best = jnp.maximum(best, ref[s])
        if s == 0:
            best = jnp.maximum(best, earlier[0][0])
        found[s] = best
    peaks = []
    for c in range(clusters):
        top = jnp.zeros((8, 128), jnp.float32)
        for s in range(SLOTS):
            top = jnp.maximum(top, jnp.where(idn_ref[s] == float(c), found[s], 0.0))
        peaks.append(jnp.max(top, axis=0, keepdims=True))
    peaks.append(jnp.zeros((128 - clusters, 128), jnp.float32))
    peak = jnp.max(jnp.concatenate(peaks, axis=0).T, axis=0, keepdims=True)
    out_ref[:, 0:8, :] = jnp.zeros((out_ref.shape[0], 8, 128), jnp.float32)
    out_ref[:, 8:9, :] = jnp.broadcast_to(peak[None], (out_ref.shape[0], 1, 128))
    for s in range(SLOTS):
        out_ref[info_ref[16 * SLOTS + s], 0:8, :] = found[s]


VMEM = pl.BlockSpec(memory_space=pltpu.VMEM)
SMEM = pl.BlockSpec(memory_space=pltpu.SMEM)
HBM = pl.BlockSpec(memory_space=pl.ANY)
PARAMS = pltpu.CompilerParams(vmem_limit_bytes=30 * 2**20)


def maxima(slots):
    return jax.ShapeDtypeStruct((slots, 8, 128), jnp.float32)


def scratch(slots):
    return [
        pltpu.VMEM((slots * ROWS, 128), jnp.float32),
        pltpu.VMEM((slots * ROWS, 128), jnp.float32),
        pltpu.VMEM((slots, 8, ROWS), jnp.float32),
    ]


def own_maxima(info, own, idr):
    return pl.pallas_call(
        own_kernel,
        out_shape=maxima(1),
        in_specs=[SMEM, VMEM, VMEM],
        out_specs=VMEM,
        scratch_shapes=scratch(1),
        compiler_params=PARAMS,
    )(info, own, idr)


def step_maxima(step, clusters, count, info, idr, own, sibling, new, old, idn, earlier):
    last = step == len(CHUNKS) - 1
    extra = [idn] + earlier if last else []
    out = jax.ShapeDtypeStruct((count, 9, 128), jnp.float32) if last else maxima(SLOTS)
    return pl.pallas_call(
        functools.partial(step_kernel, step, clusters),
        out_shape=out,
        in_specs=[SMEM] + [VMEM] * 7 + [HBM] * len(old) + [VMEM] * len(extra),
        out_specs=VMEM,
        scratch_shapes=scratch(SLOTS)
        + [pltpu.VMEM((4 * ROWS, WIDTH), jnp.bfloat16), pltpu.SemaphoreType.DMA((1,))]
        + ([pltpu.VMEM((SLOTS, 8, 128), jnp.float32)] if last else []),
        compiler_params=PARAMS,
    )(info, idr, own, sibling, *new, *old, *extra)


def local(embeddings, cluster_sizes):
    count = lax.axis_size(AXIS)
    clusters = cluster_sizes.shape[0]
    me = lax.axis_index(AXIS)
    kind = lax.rem(me, RING)
    ring = me - kind

    ends = jnp.cumsum(cluster_sizes)
    blocks = (jnp.asarray(BLOCKS)[kind] + ring) % count
    pos = blocks[:, None] * ROWS + jnp.arange(ROWS, dtype=jnp.int32)[None, :]
    ids = jnp.sum((ends[None, None, :] <= pos[:, :, None]).astype(jnp.int32), axis=2)
    spans = jnp.concatenate([ids[:, ::PIECE], ids[:, PIECE - 1 :: PIECE]], axis=1).reshape(-1)
    info = jnp.concatenate([spans, blocks, jnp.asarray(KIND_TILES)[kind]])
    idr = ids.astype(jnp.float32)[:, None, :]
    idn = ids.astype(jnp.float32).reshape(SLOTS, 8, 128)

    swap = [(i, i ^ 1) for i in range(count)]
    ways = routes(count)

    def send(part):
        return [lax.ppermute(part, AXIS, way) for way in ways]

    steps = len(CHUNKS)
    part = unit_rows(embeddings[: CHUNKS[0]])
    got = [send(part)]
    embeddings, _ = lax.optimization_barrier((embeddings, part))
    own, *parts = normalize_all(embeddings)
    got.append(send(parts[0]))
    sibling = lax.ppermute(own, AXIS, swap)
    earlier = [own_maxima(info, own, idr[:1])]
    for step in range(steps):
        r0, r1, r2 = got[step]
        if step:
            (r0, r1, r2), _ = lax.optimization_barrier(((r0, r1, r2), earlier[-1]))
        passed = jnp.where(kind == 0, r1, jnp.where((kind == 1) | (kind == 7), r2, r0))
        got[step].append(lax.ppermute(passed, AXIS, swap))
        if step + 2 < steps:
            got.append(send(parts[step + 1]))
        if step == 0:
            info, _ = lax.optimization_barrier((info, earlier[0]))
        new = got[step]
        old = [got[k][s] for s in range(4) for k in range(step)]
        result = step_maxima(
            step, clusters, count, info, idr, own, sibling, new, old, idn, earlier
        )
        earlier = earlier + [result]

    back = lax.all_to_all(result, AXIS, 0, 0, tiled=True)
    final = jnp.max(back, axis=0) * (1.0 / WIDTH)
    return final[:8].reshape(ROWS), final[8, :clusters]


def solution(mesh):
    placed = (P(AXIS, None), P())
    return jax.shard_map(
        local, mesh=mesh, in_specs=placed, out_specs=(P(AXIS), P()), check_vma=False
    )
```

time: 527 us -> 110 us (0.21)
  waiting for transfers between devices: 305 us -> 26 us
  blocking collectives: 102 us -> 30.7 us
  starting transfers between devices: 75 us -> 19.7 us
  matrix products: 37.8 us -> 0 us
  Pallas kernels: 0 us -> 23.5 us
    ppermute x16 -> x9, waiting for transfers between devices: 305 us -> 26 us  [the longest x6 23.7 us: send(): return [lax.ppermute(part, AXIS, way) for way in ways]]
    pmax x1 -> x0, blocking collectives: 102 us -> none  [local(): cluster_max = lax.pmax(local_peaks, 'docs')]
    ppermute x16 -> x9, starting transfers between devices: 75 us -> 19.7 us  [the longest x6 11.7 us: send(): return [lax.ppermute(part, AXIS, way) for way in ways]]
    dot_general x9 -> x0, matrix products: 37.8 us -> none  [tile_maxima(): lax.dot_general(left_block, right_block, (((1,), (1,)), ((), ())), prefer...]
    all_to_all x0 -> x1, blocking collectives: none -> 30.7 us  [local(): back = lax.all_to_all(result, AXIS, 0, 0, tiled=True)]
    pallas_call x0 -> x4, Pallas kernels: none -> 23.5 us  [the longest x2 14.8 us: step_maxima(): pl.pallas_call(functools.partial(step_kernel, step, clusters), out_shape=...]
  transfers between devices with their start and end apart: 16 -> 9, of which waited for: 9 -> 5; matrix products, arithmetic and copies ran while one was open for 7% -> 3% of each run, Pallas kernels for 0% -> 14%
where the time goes in v2:
time: 110 us; the launch traced here: 111 us
  blocking collectives  30.7 us (28%)
  waiting for transfers between devices  26 us (24%)
  Pallas kernels  23.5 us (21%)
  starting transfers between devices  19.7 us (18%)
  other arithmetic  7.99 us (7%)
  local copies, waits for them, and re-layouts  2.19 us (2%)
    all_to_all x1, blocking collectives, local(): back = lax.all_to_all(result, AXIS, 0, 0, tiled=True)  30.7 us
    ppermute x6, waiting for transfers between devices, send(): return [lax.ppermute(part, AXIS, way) for way in ways]  23.7 us
    pallas_call x2, Pallas kernels, step_maxima(): pl.pallas_call(functools.partial(step_kernel, step, clusters), out_shape=...  14.8 us
    ppermute x6, starting transfers between devices, send(): return [lax.ppermute(part, AXIS, way) for way in ways]  11.7 us
    pallas_call x1, Pallas kernels, own_maxima(): pl.pallas_call(own_kernel, out_shape=maxima(1), in_specs=[SMEM, VMEM, VME...  4.39 us
    pallas_call x1, Pallas kernels, normalize_all(): pl.pallas_call(norm_all_kernel, out_shape=[jax.ShapeDtypeStruct((ROWS, WI...  4.31 us
    ppermute x2, starting transfers between devices, local(): got[step].append(lax.ppermute(passed, AXIS, swap))  4.19 us
    ppermute x1, starting transfers between devices, local(): sibling = lax.ppermute(own, AXIS, swap)  3.86 us
  transfers between devices with their start and end apart: 9, of which 5 were waited for; matrix products, arithmetic and copies ran while one was open for 3% of the time, Pallas kernels for 14%

profile of v2, /device:TPU:1, one launch (start us, length us, event | category | flops | bytes accessed | tf_op | source)
XLA Modules:
  0.0 110.8 jit_solution(7812367395778137626)
XLA Ops:
  0.6 1.5 %fusion = f32[512]{0:T(512)S(1)} fusion(bf16[1024,1024]{1,0:T(8,128)(2,1)} %x_ref), kind=kLoop, calls=%fused_computation.2 | loop fusion | flops 1572352 | bytes 1050624 | tf_op jit(solution)/shard_map/reduce_sum | solution.py:96
  2.2 2.4 %fusion.1 = bf16[512,1024]{1,0:T(8,128)(2,1)} fusion(f32[512]{0:T(512)S(1)} %add_rsqrt_fusion, bf16[1024,1024]{1,0:T(8,128)(2,1)} %x_ref), kind=kLoop, calls=%fused_computation.3 | loop fusion | flops 1572864 | bytes 2099200 | tf_op jit(solution)/shard_map/convert_element_type | solution.py:97
  4.6 6.3 %collective-permute-start.6 = (bf16[512,1024]{1,0:T(8,128)(2,1)}, bf16[512,1024]{1,0:T(8,128)(2,1)S(1)}, u32[]{:S(2)}, u32[]{:S(2)}) collective-permute-start(bf16[512,1024]{1,0:T(8,128)(2,1)} %fusion.1), channel_id=1, source_target_pairs={{9,0},{7,1},{122,2},{0,3},{11,4},{13,5},{14,6},{4,7},{17,8},{15,9}... | collective-permute-start | bytes 3145736 | tf_op jit(solution)/shard_map/ppermute | solution.py:365
  10.9 0.6 collective-permute-start.4
  11.5 4.3 %shard_map.59 = (bf16[1024,1024]{1,0:T(8,128)(2,1)}, bf16[512,1024]{1,0:T(8,128)(2,1)}) custom-call(bf16[1024,1024]{1,0:T(8,128)(2,1)} %x_ref), custom_call_target="tpu_custom_call" | custom-call | tf_op jit(solution)/shard_map/pallas_call | solution.py:119
  15.8 3.9 %collective-permute-start = (bf16[1024,1024]{1,0:T(8,128)(2,1)}, bf16[1024,1024]{1,0:T(8,128)(2,1)}, u32[]{:S(2)}, u32[]{:S(2)}) collective-permute-start(bf16[1024,1024]{1,0:T(8,128)(2,1)} %get-tuple-element.10.own_ref), channel_id=1, source_target_pairs={{0,1},{1,0},{2,3},{3,2},{4,5},{5,4},{6,7},{7,6},{8,9},{9,8},{10,11... | collective-permute-start | bytes 6291464 | tf_op jit(solution)/shard_map/ppermute | solution.py:373
  19.7 4.8 %collective-permute-start.3 = (bf16[512,1024]{1,0:T(8,128)(2,1)}, bf16[512,1024]{1,0:T(8,128)(2,1)}, u32[]{:S(2)}, u32[]{:S(2)}) collective-permute-start(bf16[512,1024]{1,0:T(8,128)(2,1)} %get-tuple-element.12), channel_id=1, source_target_pairs={{9,0},{7,1},{122,2},{0,3},{11,4},{13,5},{14,6},{4,7},{17,8},{15,9}... | collective-permute-start | bytes 3145736 | tf_op jit(solution)/shard_map/ppermute | solution.py:365
  24.8 0.7 broadcast_multiply_fusion.1
  25.5 7.6 %collective-permute-done.6.refs_2_.refs_6_ = bf16[512,1024]{1,0:T(8,128)(2,1)S(1)} collective-permute-done((bf16[512,1024]{1,0:T(8,128)(2,1)}, bf16[512,1024]{1,0:T(8,128)(2,1)S(1)}, u32[]{:S(2)}, u32[]{:S(2)}) %collective-permute-start.6) | collective-permute-done | bytes 1048608 | tf_op jit(solution)/shard_map/ppermute | solution.py:365
  33.1 4.0 %collective-permute-done.5.refs_1_.refs_5_ = bf16[512,1024]{1,0:T(8,128)(2,1)} collective-permute-done((bf16[512,1024]{1,0:T(8,128)(2,1)}, bf16[512,1024]{1,0:T(8,128)(2,1)}, u32[]{:S(2)}, u32[]{:S(2)}) %collective-permute-start.5) | collective-permute-done | bytes 1048608 | tf_op jit(solution)/shard_map/ppermute | solution.py:365
  37.1 1.0 collective-permute-done.4.refs_0_.refs_4_
  38.0 1.1 %select_select_fusion.1 = bf16[512,1024]{1,0:T(8,128)(2,1)} fusion(bf16[512,1024]{1,0:T(8,128)(2,1)} %collective-permute-done.5.refs_1_.refs_5_, bf16[512,1024]{1,0:T(8,128)(2,1)S(1)} %collective-permute-done.6.refs_2_.refs_6_, bf16[512,1024]{1,0:T(8,128)(2,1)} %collective-permute-done.4.refs_0_.refs_4_, pred[]{:T(512)S(6)} %or.4, pred[]{:T(512)S(6)} %eq.14), kind=kLoop, calls=%fused_computation.6 | loop fusion | flops 1048576 | bytes 4194306 | tf_op jit(solution)/shard_map/jit(_where)/select_n | solution.py:379
  39.1 3.3 %collective-permute-start.7 = (bf16[512,1024]{1,0:T(8,128)(2,1)}, bf16[512,1024]{1,0:T(8,128)(2,1)}, u32[]{:S(2)}, u32[]{:S(2)}) collective-permute-start(bf16[512,1024]{1,0:T(8,128)(2,1)} %select_select_fusion.1), channel_id=1, source_target_pairs={{0,1},{1,0},{2,3},{3,2},{4,5},{5,4},{6,7},{7,6},{8,9},{9,8},{10,11... | collective-permute-start | bytes 3145736 | tf_op jit(solution)/shard_map/ppermute | solution.py:380
  43.1 0.7 dynamic-slice_bitcast_fusion
  43.9 4.4 %shard_map.60.refs_9_ = f32[1,8,128]{2,1,0:T(8,128)S(1)} custom-call(s32[123]{0:T(128)S(1)} %pad_add_fusion.1.info_ref, bf16[1024,1024]{1,0:T(8,128)(2,1)S(1)} %copy-done, f32[1,1,1024]{2,1,0:T(1,128)S(1)} %slice_bitcast_fusion.1.idr_ref), custom_call_target="tpu_custom_call" | custom-call | tf_op jit(solution)/shard_map/pallas_call | solution.py:319
  48.3 7.1 %shard_map.61.refs_10_ = f32[6,8,128]{2,1,0:T(8,128)S(1)} custom-call(s32[123]{0:T(128)S(1)} %pad_add_fusion.1.info_ref, f32[6,1,1024]{2,1,0:T(1,128)S(1)} %convert_element_type.31.idr_ref, bf16[1024,1024]{1,0:T(8,128)(2,1)S(1)} %copy-done, bf16[1024,1024]{1,0:T(8,128)(2,1)} %collective-permute-done.sib_ref, ...), custom_call_target="tpu_custom_call" | custom-call | tf_op jit(solution)/shard_map/pallas_call | solution.py:333
  55.5 11.2 %collective-permute-done.1.refs_0_ = bf16[512,1024]{1,0:T(8,128)(2,1)} collective-permute-done((bf16[512,1024]{1,0:T(8,128)(2,1)}, bf16[512,1024]{1,0:T(8,128)(2,1)}, u32[]{:S(2)}, u32[]{:S(2)}) %collective-permute-start.1) | collective-permute-done | bytes 1048608 | tf_op jit(solution)/shard_map/ppermute | solution.py:365
  66.6 1.4 %select_select_fusion = bf16[512,1024]{1,0:T(8,128)(2,1)S(1)} fusion(bf16[512,1024]{1,0:T(8,128)(2,1)} %collective-permute-done.2.refs_1_, bf16[512,1024]{1,0:T(8,128)(2,1)} %collective-permute-done.3.refs_2_, bf16[512,1024]{1,0:T(8,128)(2,1)} %collective-permute-done.1.refs_0_, pred[]{:T(512)S(6)} %or.4, pred[]{:T(512)S(6)} %eq.14), kind=kLoop, calls=%fused_computation.5 | loop fusion | flops 1048576 | bytes 4194306 | tf_op jit(solution)/shard_map/jit(_where)/select_n | solution.py:379
  68.0 0.9 collective-permute-start.8
  68.9 2.3 %collective-permute-done.8.refs_3_ = bf16[512,1024]{1,0:T(8,128)(2,1)S(1)} collective-permute-done((bf16[512,1024]{1,0:T(8,128)(2,1)S(1)}, bf16[512,1024]{1,0:T(8,128)(2,1)S(1)}, u32[]{:S(2)}, u32[]{:S(2)}) %collective-permute-start.8) | collective-permute-done | bytes 1048608 | tf_op jit(solution)/shard_map/ppermute | solution.py:380
  71.2 7.7 %shard_map.62 = f32[128,9,128]{2,1,0:T(8,128)S(1)} custom-call(s32[123]{0:T(128)S(1)} %pad_add_fusion.1.info_ref, f32[6,1,1024]{2,1,0:T(1,128)S(1)} %convert_element_type.31.idr_ref, bf16[1024,1024]{1,0:T(8,128)(2,1)S(1)} %copy-done, bf16[1024,1024]{1,0:T(8,128)(2,1)} %collective-permute-done.sib_ref, bf16[512,1024]{1,0:T(8,128)(2,1)} %collective-permute-done.1.refs_0_, ...), custom_call_target="tpu_custom_call" | custom-call | tf_op jit(solution)/shard_map/pallas_call | solution.py:333
  78.9 30.7 %all_to_all.5 = f32[128,9,128]{2,1,0:T(8,128)S(1)} all-to-all(f32[128,9,128]{2,1,0:T(8,128)S(1)} %shard_map.62), channel_id=1, replica_groups=mesh['docs'=128] {'docs'}, dimensions={0} | all-to-all | bytes 1179648 | tf_op jit(solution)/shard_map/all_to_all | solution.py:392
  109.7 0.5 slice_bitcast_fusion.2
  110.2 0.6 slice_bitcast_fusion
  (28 shorter events, 1.3 us)
Async XLA Ops:
  2.1 22.3 %copy-start.1 = (s32[64]{0:T(128)S(1)}, s32[64]{0:T(128)}, u32[]{:S(2)}) copy-start(s32[64]{0:T(128)} %param.5) | copy-start | bytes 772
  4.6 28.5 %collective-permute-start.6 = (bf16[512,1024]{1,0:T(8,128)(2,1)}, bf16[512,1024]{1,0:T(8,128)(2,1)S(1)}, u32[]{:S(2)}, u32[]{:S(2)}) collective-permute-start(bf16[512,1024]{1,0:T(8,128)(2,1)} %fusion.1), channel_id=1, source_target_pairs={{9,0},{7,1},{122,2},{0,3},{11,4},{13,5},{14,6},{4,7},{17,8},{15,9}... | collective-permute-start | bytes 3145736 | tf_op jit(solution)/shard_map/ppermute | solution.py:365
  10.9 26.1 %collective-permute-start.5 = (bf16[512,1024]{1,0:T(8,128)(2,1)}, bf16[512,1024]{1,0:T(8,128)(2,1)}, u32[]{:S(2)}, u32[]{:S(2)}) collective-permute-start(bf16[512,1024]{1,0:T(8,128)(2,1)} %fusion.1), channel_id=1, source_target_pairs={{6,0},{8,1},{1,2},{123,3},{10,4},{12,5},{127,6},{125,7},{14,8},{16... | collective-permute-start | bytes 3145736 | tf_op jit(solution)/shard_map/ppermute | solution.py:365
  10.9 27.1 %collective-permute-start.4 = (bf16[512,1024]{1,0:T(8,128)(2,1)}, bf16[512,1024]{1,0:T(8,128)(2,1)}, u32[]{:S(2)}, u32[]{:S(2)}) collective-permute-start(bf16[512,1024]{1,0:T(8,128)(2,1)} %fusion.1), channel_id=1, source_target_pairs={{3,0},{2,1},{124,2},{5,3},{6,4},{7,5},{0,6},{1,7},{11,8},{10,9},{4... | collective-permute-start | bytes 3145736 | tf_op jit(solution)/shard_map/ppermute | solution.py:365
  15.8 32.5 %collective-permute-start = (bf16[1024,1024]{1,0:T(8,128)(2,1)}, bf16[1024,1024]{1,0:T(8,128)(2,1)}, u32[]{:S(2)}, u32[]{:S(2)}) collective-permute-start(bf16[1024,1024]{1,0:T(8,128)(2,1)} %get-tuple-element.10.own_ref), channel_id=1, source_target_pairs={{0,1},{1,0},{2,3},{3,2},{4,5},{5,4},{6,7},{7,6},{8,9},{9,8},{10,11... | collective-permute-start | bytes 6291464 | tf_op jit(solution)/shard_map/ppermute | solution.py:373
  19.7 35.8 %collective-permute-start.3 = (bf16[512,1024]{1,0:T(8,128)(2,1)}, bf16[512,1024]{1,0:T(8,128)(2,1)}, u32[]{:S(2)}, u32[]{:S(2)}) collective-permute-start(bf16[512,1024]{1,0:T(8,128)(2,1)} %get-tuple-element.12), channel_id=1, source_target_pairs={{9,0},{7,1},{122,2},{0,3},{11,4},{13,5},{14,6},{4,7},{17,8},{15,9}... | collective-permute-start | bytes 3145736 | tf_op jit(solution)/shard_map/ppermute | solution.py:365
  25.5 18.4 %copy-start = (bf16[1024,1024]{1,0:T(8,128)(2,1)S(1)}, bf16[1024,1024]{1,0:T(8,128)(2,1)}, u32[]{:S(2)}) copy-start(bf16[1024,1024]{1,0:T(8,128)(2,1)} %get-tuple-element.10.own_ref) | copy-start | bytes 6291460
  33.1 22.4 %collective-permute-start.2 = (bf16[512,1024]{1,0:T(8,128)(2,1)}, bf16[512,1024]{1,0:T(8,128)(2,1)}, u32[]{:S(2)}, u32[]{:S(2)}) collective-permute-start(bf16[512,1024]{1,0:T(8,128)(2,1)} %get-tuple-element.12), channel_id=1, source_target_pairs={{6,0},{8,1},{1,2},{123,3},{10,4},{12,5},{127,6},{125,7},{14,8},{16... | collective-permute-start | bytes 3145736 | tf_op jit(solution)/shard_map/ppermute | solution.py:365
  37.1 29.6 %collective-permute-start.1 = (bf16[512,1024]{1,0:T(8,128)(2,1)}, bf16[512,1024]{1,0:T(8,128)(2,1)}, u32[]{:S(2)}, u32[]{:S(2)}) collective-permute-start(bf16[512,1024]{1,0:T(8,128)(2,1)} %get-tuple-element.12), channel_id=1, source_target_pairs={{3,0},{2,1},{124,2},{5,3},{6,4},{7,5},{0,6},{1,7},{11,8},{10,9},{4... | collective-permute-start | bytes 3145736 | tf_op jit(solution)/shard_map/ppermute | solution.py:365
  39.1 9.2 %collective-permute-start.7 = (bf16[512,1024]{1,0:T(8,128)(2,1)}, bf16[512,1024]{1,0:T(8,128)(2,1)}, u32[]{:S(2)}, u32[]{:S(2)}) collective-permute-start(bf16[512,1024]{1,0:T(8,128)(2,1)} %select_select_fusion.1), channel_id=1, source_target_pairs={{0,1},{1,0},{2,3},{3,2},{4,5},{5,4},{6,7},{7,6},{8,9},{9,8},{10,11... | collective-permute-start | bytes 3145736 | tf_op jit(solution)/shard_map/ppermute | solution.py:380
  68.0 3.2 %collective-permute-start.8 = (bf16[512,1024]{1,0:T(8,128)(2,1)S(1)}, bf16[512,1024]{1,0:T(8,128)(2,1)S(1)}, u32[]{:S(2)}, u32[]{:S(2)}) collective-permute-start(bf16[512,1024]{1,0:T(8,128)(2,1)S(1)} %select_select_fusion), channel_id=1, source_target_pairs={{0,1},{1,0},{2,3},{3,2},{4,5},{5,4},{6,7},{7,6},{8,9},{9,8},{10,11... | collective-permute-start | bytes 3145736 | tf_op jit(solution)/shard_map/ppermute | solution.py:380

commit v3 on v2

--- a/solution.py
+++ b/solution.py
@@ -93,8 +93,31 @@
 
 def unit_rows(v):
     v = v.astype(jnp.float32)
-    mean = jnp.sum(v * v, axis=1, keepdims=True) * (1.0 / WIDTH)
-    return (v * lax.rsqrt(mean + 1e-06)).astype(jnp.bfloat16)
+    square = v * v
+    high = square.astype(jnp.bfloat16)
+    low = (square - high.astype(jnp.float32)).astype(jnp.bfloat16)
+    ones = jnp.ones((WIDTH, 128), jnp.bfloat16)
+    total = jnp.dot(high, ones, preferred_element_type=jnp.float32)
+    total += jnp.dot(low, ones, preferred_element_type=jnp.float32)
+    scale = lax.rsqrt(total * (1.0 / WIDTH) + 1e-06)
+    return jnp.concatenate(
+        [v[:, g : g + 128] * scale for g in range(0, WIDTH, 128)], axis=1
+    ).astype(jnp.bfloat16)
+
+
+def norm_kernel(x_ref, out_ref):
+    out_ref[...] = unit_rows(x_ref[...])
+
+
+def normalize_first(embeddings):
+    block = pl.BlockSpec((STRIP, WIDTH), lambda i: (i, 0))
+    return pl.pallas_call(
+        norm_kernel,
+        out_shape=jax.ShapeDtypeStruct((CHUNKS[0], WIDTH), jnp.bfloat16),
+        grid=(CHUNKS[0] // STRIP,),
+        in_specs=[block],
+        out_specs=block,
+    )(embeddings)
 
 
 def norm_all_kernel(x_ref, own_ref, *part_refs):
@@ -169,12 +192,13 @@
         self.accr[rows, :] = best
 
     def finish(self, slot, out):
-        lanes = self.accr[slot * ROWS : (slot + 1) * ROWS, :]
-        best = jnp.max(lanes.T.reshape(128, 8, 128), axis=0)
         cols = jnp.max(self.accc[slot], axis=0, keepdims=True)
         for v in range(8):
-            out[slot, v : v + 1, :] = jnp.maximum(
-                best[v : v + 1], cols[:, v * 128 : (v + 1) * 128]
+            out[slot, v : v + 1, :] = cols[:, v * 128 : (v + 1) * 128]
+        if (slot + 1) * ROWS <= self.accr.shape[0]:
+            lanes = self.accr[slot * ROWS : (slot + 1) * ROWS, :]
+            out[slot] = jnp.maximum(
+                out[slot], jnp.max(lanes.T.reshape(128, 8, 128), axis=0)
             )
 
 
@@ -307,10 +331,10 @@
     return jax.ShapeDtypeStruct((slots, 8, 128), jnp.float32)
 
 
-def scratch(slots):
+def scratch(slots, rows):
     return [
-        pltpu.VMEM((slots * ROWS, 128), jnp.float32),
-        pltpu.VMEM((slots * ROWS, 128), jnp.float32),
+        pltpu.VMEM((rows * ROWS, 128), jnp.float32),
+        pltpu.VMEM((rows * ROWS, 128), jnp.float32),
         pltpu.VMEM((slots, 8, ROWS), jnp.float32),
     ]
 
@@ -321,7 +345,7 @@
         out_shape=maxima(1),
         in_specs=[SMEM, VMEM, VMEM],
         out_specs=VMEM,
-        scratch_shapes=scratch(1),
+        scratch_shapes=scratch(1, 1),
         compiler_params=PARAMS,
     )(info, own, idr)
 
@@ -335,7 +359,7 @@
         out_shape=out,
         in_specs=[SMEM] + [VMEM] * 7 + [HBM] * len(old) + [VMEM] * len(extra),
         out_specs=VMEM,
-        scratch_shapes=scratch(SLOTS)
+        scratch_shapes=scratch(SLOTS, SLOTS - 1)
         + [pltpu.VMEM((4 * ROWS, WIDTH), jnp.bfloat16), pltpu.SemaphoreType.DMA((1,))]
         + ([pltpu.VMEM((SLOTS, 8, 128), jnp.float32)] if last else []),
         compiler_params=PARAMS,
@@ -365,7 +389,7 @@
         return [lax.ppermute(part, AXIS, way) for way in ways]
 
     steps = len(CHUNKS)
-    part = unit_rows(embeddings[: CHUNKS[0]])
+    part = normalize_first(embeddings)
     got = [send(part)]
     embeddings, _ = lax.optimization_barrier((embeddings, part))
     own, *parts = normalize_all(embeddings)
@@ -373,15 +397,16 @@
     sibling = lax.ppermute(own, AXIS, swap)
     earlier = [own_maxima(info, own, idr[:1])]
     for step in range(steps):
+        if step:
+            got[step], _ = lax.optimization_barrier((got[step], earlier[-1]))
+            got[step] = list(got[step])
+        choice = jnp.asarray(PASSED, jnp.int32)[kind]
         r0, r1, r2 = got[step]
-        if step:
-            (r0, r1, r2), _ = lax.optimization_barrier(((r0, r1, r2), earlier[-1]))
-        passed = jnp.where(kind == 0, r1, jnp.where((kind == 1) | (kind == 7), r2, r0))
+        passed = jnp.where(choice == 1, r1, jnp.where(choice == 2, r2, r0))
+        info, _ = lax.optimization_barrier((info, earlier[-1]))
         got[step].append(lax.ppermute(passed, AXIS, swap))
         if step + 2 < steps:
             got.append(send(parts[step + 1]))
-        if step == 0:
-            info, _ = lax.optimization_barrier((info, earlier[0]))
         new = got[step]
         old = [got[k][s] for s in range(4) for k in range(step)]
         result = step_maxima(
@@ -390,8 +415,8 @@
         earlier = earlier + [result]
 
     back = lax.all_to_all(result, AXIS, 0, 0, tiled=True)
-    final = jnp.max(back, axis=0) * (1.0 / WIDTH)
-    return final[:8].reshape(ROWS), final[8, :clusters]
+    rows = jnp.max(back[:, :8, :], axis=0) * (1.0 / WIDTH)
+    return rows.reshape(ROWS), jnp.max(back[:, 8, :clusters], axis=0) * (1.0 / WIDTH)
 
 
 def solution(mesh):

time: 110 us -> 108 us (0.982)
  waiting for transfers between devices: 26 us -> 22.9 us
  other arithmetic: 7.99 us -> 5.3 us
  Pallas kernels: 23.5 us -> 25.4 us
  between operations: 0.75 us -> 2.07 us
    ppermute x6, waiting for transfers between devices: 23.7 us -> 20.7 us  [send(): return [lax.ppermute(part, AXIS, way) for way in ways]]
    pallas_call x0 -> x1, Pallas kernels: none -> 2.87 us  [normalize_first(): pl.pallas_call(norm_kernel, out_shape=jax.ShapeDtypeStruct((CHUNKS[0], WI...]
    convert_element_type x1 -> x0, other arithmetic: 2.45 us -> none  [unit_rows(): return (v * lax.rsqrt(mean + 1e-06)).astype(jnp.bfloat16)]
    reduce_sum x1 -> x0, other arithmetic: 1.5 us -> none  [unit_rows(): mean = jnp.sum(v * v, axis=1, keepdims=True) * (1.0 / WIDTH)]
    pallas_call x2, Pallas kernels: 14.8 us -> 13.3 us  [step_maxima(): pl.pallas_call(functools.partial(step_kernel, step, clusters), out_shape=...]
    mul x1 -> x2, other arithmetic: 0.01 us -> 1.11 us  [the longest x1 0.6 us: local(): rows = jnp.max(back[:, :8, :], axis=0) * (1.0 / WIDTH)]
  transfers between devices with their start and end apart: 9 -> 9, of which waited for: 5 -> 5; matrix products, arithmetic and copies ran while one was open for 3% -> 4% of each run, Pallas kernels for 14% -> 14%
where the time goes in v3:
time: 108 us; the launch traced here: 109 us
  blocking collectives  30.2 us (28%)
  Pallas kernels  25.4 us (24%)
  waiting for transfers between devices  22.9 us (21%)
  starting transfers between devices  20.1 us (19%)
  other arithmetic  5.3 us (5%)
  local copies, waits for them, and re-layouts  2.8 us (3%)
  between operations  2.07 us (2%)
    all_to_all x1, blocking collectives, local(): back = lax.all_to_all(result, AXIS, 0, 0, tiled=True)  30.2 us
    ppermute x6, waiting for transfers between devices, send(): return [lax.ppermute(part, AXIS, way) for way in ways]  20.7 us
    pallas_call x2, Pallas kernels, step_maxima(): pl.pallas_call(functools.partial(step_kernel, step, clusters), out_shape=...  13.3 us
    ppermute x6, starting transfers between devices, send(): return [lax.ppermute(part, AXIS, way) for way in ways]  11.7 us
    pallas_call x1, Pallas kernels, normalize_all(): pl.pallas_call(norm_all_kernel, out_shape=[jax.ShapeDtypeStruct((ROWS, WI...  4.9 us
    ppermute x2, starting transfers between devices, local(): got[step].append(lax.ppermute(passed, AXIS, swap))  4.55 us
    pallas_call x1, Pallas kernels, own_maxima(): pl.pallas_call(own_kernel, out_shape=maxima(1), in_specs=[SMEM, VMEM, VME...  4.38 us
    ppermute x1, starting transfers between devices, local(): sibling = lax.ppermute(own, AXIS, swap)  3.86 us
  transfers between devices with their start and end apart: 9, of which 5 were waited for; matrix products, arithmetic and copies ran while one was open for 4% of the time, Pallas kernels for 14%

profile of v3, /device:TPU:1, one launch (start us, length us, event | category | flops | bytes accessed | tf_op | source)
XLA Modules:
  0.0 108.8 jit_solution(2309563747024851222)
XLA Ops:
  0.7 2.9 %shard_map.77 = bf16[512,1024]{1,0:T(8,128)(2,1)} custom-call(bf16[1024,1024]{1,0:T(8,128)(2,1)} %x_ref.2), custom_call_target="tpu_custom_call" | custom-call | tf_op jit(solution)/shard_map/pallas_call | solution.py:114
  3.5 6.3 %collective-permute-start.3 = (bf16[512,1024]{1,0:T(8,128)(2,1)}, bf16[512,1024]{1,0:T(8,128)(2,1)S(1)}, u32[]{:S(2)}, u32[]{:S(2)}) collective-permute-start(bf16[512,1024]{1,0:T(8,128)(2,1)} %shard_map.77), channel_id=1, source_target_pairs={{9,0},{7,1},{122,2},{0,3},{11,4},{13,5},{14,6},{4,7},{17,8},{15,9}... | collective-permute-start | bytes 3145736 | tf_op jit(solution)/shard_map/ppermute | solution.py:389
  9.8 0.6 collective-permute-start.1
  10.4 4.9 %shard_map.78 = (bf16[1024,1024]{1,0:T(8,128)(2,1)}, bf16[512,1024]{1,0:T(8,128)(2,1)}) custom-call(bf16[1024,1024]{1,0:T(8,128)(2,1)} %x_ref.2), custom_call_target="tpu_custom_call" | custom-call | tf_op jit(solution)/shard_map/pallas_call | solution.py:142
  15.3 3.9 %collective-permute-start = (bf16[1024,1024]{1,0:T(8,128)(2,1)}, bf16[1024,1024]{1,0:T(8,128)(2,1)}, u32[]{:S(2)}, u32[]{:S(2)}) collective-permute-start(bf16[1024,1024]{1,0:T(8,128)(2,1)} %get-tuple-element.11.own_ref), channel_id=1, source_target_pairs={{0,1},{1,0},{2,3},{3,2},{4,5},{5,4},{6,7},{7,6},{8,9},{9,8},{10,11... | collective-permute-start | bytes 6291464 | tf_op jit(solution)/shard_map/ppermute | solution.py:397
  19.2 4.8 %collective-permute-start.7 = (bf16[512,1024]{1,0:T(8,128)(2,1)}, bf16[512,1024]{1,0:T(8,128)(2,1)}, u32[]{:S(2)}, u32[]{:S(2)}) collective-permute-start(bf16[512,1024]{1,0:T(8,128)(2,1)} %get-tuple-element.14), channel_id=1, source_target_pairs={{9,0},{7,1},{122,2},{0,3},{11,4},{13,5},{14,6},{4,7},{17,8},{15,9}... | collective-permute-start | bytes 3145736 | tf_op jit(solution)/shard_map/ppermute | solution.py:389
  24.0 0.6 dynamic_slice.14
  26.2 0.7 broadcast_multiply_fusion.1
  26.9 5.1 %collective-permute-done.3.refs_2_.refs_6_ = bf16[512,1024]{1,0:T(8,128)(2,1)S(1)} collective-permute-done((bf16[512,1024]{1,0:T(8,128)(2,1)}, bf16[512,1024]{1,0:T(8,128)(2,1)S(1)}, u32[]{:S(2)}, u32[]{:S(2)}) %collective-permute-start.3) | collective-permute-done | bytes 1048608 | tf_op jit(solution)/shard_map/ppermute | solution.py:389
  32.0 4.0 %collective-permute-done.2.refs_1_.refs_5_ = bf16[512,1024]{1,0:T(8,128)(2,1)S(1)} collective-permute-done((bf16[512,1024]{1,0:T(8,128)(2,1)}, bf16[512,1024]{1,0:T(8,128)(2,1)S(1)}, u32[]{:S(2)}, u32[]{:S(2)}) %collective-permute-start.2) | collective-permute-done | bytes 1048608 | tf_op jit(solution)/shard_map/ppermute | solution.py:389
  36.0 1.0 collective-permute-done.1.refs_0_.refs_4_
  36.9 1.0 copy-done.3
  37.9 1.1 %select_select_fusion.1 = bf16[512,1024]{1,0:T(8,128)(2,1)} fusion(bf16[512,1024]{1,0:T(8,128)(2,1)} %copy-done.1, bf16[512,1024]{1,0:T(8,128)(2,1)S(1)} %collective-permute-done.3.refs_2_.refs_6_, bf16[512,1024]{1,0:T(8,128)(2,1)} %copy-done.3, pred[]{:T(512)} %bitcast.5, pred[]{:T(512)} %bitcast.4), kind=kLoop, calls=%fused_computation.2 | loop fusion | flops 1048576 | bytes 4194306 | tf_op jit(solution)/shard_map/jit(_where)/select_n | solution.py:405
  39.0 3.7 %collective-permute-start.4 = (bf16[512,1024]{1,0:T(8,128)(2,1)}, bf16[512,1024]{1,0:T(8,128)(2,1)}, u32[]{:S(2)}, u32[]{:S(2)}) collective-permute-start(bf16[512,1024]{1,0:T(8,128)(2,1)} %select_select_fusion.1), channel_id=1, source_target_pairs={{0,1},{1,0},{2,3},{3,2},{4,5},{5,4},{6,7},{7,6},{8,9},{9,8},{10,11... | collective-permute-start | bytes 3145736 | tf_op jit(solution)/shard_map/ppermute | solution.py:407
  43.4 0.8 dynamic-slice_bitcast_fusion
  44.3 4.4 %shard_map.79.refs_9_ = f32[1,8,128]{2,1,0:T(8,128)S(1)} custom-call(s32[123]{0:T(128)S(1)} %pad_add_fusion.1.info_ref, bf16[1024,1024]{1,0:T(8,128)(2,1)S(1)} %copy-done, f32[1,1,1024]{2,1,0:T(1,128)S(1)} %slice_bitcast_fusion.idr_ref), custom_call_target="tpu_custom_call" | custom-call | tf_op jit(solution)/shard_map/pallas_call | solution.py:343
  48.8 6.2 %shard_map.80.refs_10_ = f32[6,8,128]{2,1,0:T(8,128)S(1)} custom-call(s32[123]{0:T(128)S(1)} %pad_add_fusion.1.info_ref, f32[6,1,1024]{2,1,0:T(1,128)S(1)} %convert_element_type.23.idr_ref, bf16[1024,1024]{1,0:T(8,128)(2,1)S(1)} %copy-done, bf16[1024,1024]{1,0:T(8,128)(2,1)} %collective-permute-done.sib_ref, bf16[512,1024]{1,0:T(8,128)(2,1)S(1)} %copy-done.4, ...), custom_call_target="tpu_custom_call" | custom-call | tf_op jit(solution)/shard_map/pallas_call | solution.py:357
  55.0 10.6 %collective-permute-done.5.refs_0_ = bf16[512,1024]{1,0:T(8,128)(2,1)} collective-permute-done((bf16[512,1024]{1,0:T(8,128)(2,1)}, bf16[512,1024]{1,0:T(8,128)(2,1)}, u32[]{:S(2)}, u32[]{:S(2)}) %collective-permute-start.5) | collective-permute-done | bytes 1048608 | tf_op jit(solution)/shard_map/ppermute | solution.py:389
  65.6 1.4 %select_select_fusion = bf16[512,1024]{1,0:T(8,128)(2,1)S(1)} fusion(bf16[512,1024]{1,0:T(8,128)(2,1)} %collective-permute-done.6.refs_1_, bf16[512,1024]{1,0:T(8,128)(2,1)} %collective-permute-done.7.refs_2_, bf16[512,1024]{1,0:T(8,128)(2,1)} %collective-permute-done.5.refs_0_, pred[]{:T(512)} %bitcast.5, pred[]{:T(512)} %bitcast.4), kind=kLoop, calls=%fused_computation.1 | loop fusion | flops 1048576 | bytes 4194306 | tf_op jit(solution)/shard_map/jit(_where)/select_n | solution.py:405
  66.9 0.9 collective-permute-start.8
  67.8 2.3 %collective-permute-done.8.refs_3_ = bf16[512,1024]{1,0:T(8,128)(2,1)S(1)} collective-permute-done((bf16[512,1024]{1,0:T(8,128)(2,1)S(1)}, bf16[512,1024]{1,0:T(8,128)(2,1)S(1)}, u32[]{:S(2)}, u32[]{:S(2)}) %collective-permute-start.8) | collective-permute-done | bytes 1048608 | tf_op jit(solution)/shard_map/ppermute | solution.py:407
  70.1 7.1 %shard_map.81 = f32[128,9,128]{2,1,0:T(8,128)S(1)} custom-call(s32[123]{0:T(128)S(1)} %pad_add_fusion.1.info_ref, f32[6,1,1024]{2,1,0:T(1,128)S(1)} %convert_element_type.23.idr_ref, bf16[1024,1024]{1,0:T(8,128)(2,1)S(1)} %copy-done, bf16[1024,1024]{1,0:T(8,128)(2,1)} %collective-permute-done.sib_ref, bf16[512,1024]{1,0:T(8,128)(2,1)} %collective-permute-done.5.refs_0_, ...), custom_call_target="tpu_custom_call" | custom-call | tf_op jit(solution)/shard_map/pallas_call | solution.py:357
  77.2 30.2 %all_to_all.5 = f32[128,9,128]{2,1,0:T(8,128)S(1)} all-to-all(f32[128,9,128]{2,1,0:T(8,128)S(1)} %shard_map.81), channel_id=1, replica_groups=mesh['docs'=128] {'docs'}, dimensions={0} | all-to-all | bytes 1179648 | tf_op jit(solution)/shard_map/all_to_all | solution.py:417
  107.6 0.6 multiply_bitcast_fusion
  (37 shorter events, 1.9 us)
Async XLA Ops:
  0.6 23.3 %copy-start.6 = (s32[8]{0:T(128)S(1)}, s32[8]{0:T(128)}, u32[]{:S(2)}) copy-start(s32[8]{0:T(128)} %constant.53.clone) | copy-start | bytes 100
  0.6 25.2 %copy-start.5 = (s32[64]{0:T(128)S(1)}, s32[64]{0:T(128)}, u32[]{:S(2)}) copy-start(s32[64]{0:T(128)} %param.7) | copy-start | bytes 772
  3.5 28.5 %collective-permute-start.3 = (bf16[512,1024]{1,0:T(8,128)(2,1)}, bf16[512,1024]{1,0:T(8,128)(2,1)S(1)}, u32[]{:S(2)}, u32[]{:S(2)}) collective-permute-start(bf16[512,1024]{1,0:T(8,128)(2,1)} %shard_map.77), channel_id=1, source_target_pairs={{9,0},{7,1},{122,2},{0,3},{11,4},{13,5},{14,6},{4,7},{17,8},{15,9}... | collective-permute-start | bytes 3145736 | tf_op jit(solution)/shard_map/ppermute | solution.py:389
  9.8 26.1 %collective-permute-start.2 = (bf16[512,1024]{1,0:T(8,128)(2,1)}, bf16[512,1024]{1,0:T(8,128)(2,1)S(1)}, u32[]{:S(2)}, u32[]{:S(2)}) collective-permute-start(bf16[512,1024]{1,0:T(8,128)(2,1)} %shard_map.77), channel_id=1, source_target_pairs={{6,0},{8,1},{1,2},{123,3},{10,4},{12,5},{127,6},{125,7},{14,8},{16... | collective-permute-start | bytes 3145736 | tf_op jit(solution)/shard_map/ppermute | solution.py:389
  9.8 27.1 %collective-permute-start.1 = (bf16[512,1024]{1,0:T(8,128)(2,1)}, bf16[512,1024]{1,0:T(8,128)(2,1)S(1)}, u32[]{:S(2)}, u32[]{:S(2)}) collective-permute-start(bf16[512,1024]{1,0:T(8,128)(2,1)} %shard_map.77), channel_id=1, source_target_pairs={{3,0},{2,1},{124,2},{5,3},{6,4},{7,5},{0,6},{1,7},{11,8},{10,9},{4... | collective-permute-start | bytes 3145736 | tf_op jit(solution)/shard_map/ppermute | solution.py:389
  15.3 33.4 %collective-permute-start = (bf16[1024,1024]{1,0:T(8,128)(2,1)}, bf16[1024,1024]{1,0:T(8,128)(2,1)}, u32[]{:S(2)}, u32[]{:S(2)}) collective-permute-start(bf16[1024,1024]{1,0:T(8,128)(2,1)} %get-tuple-element.11.own_ref), channel_id=1, source_target_pairs={{0,1},{1,0},{2,3},{3,2},{4,5},{5,4},{6,7},{7,6},{8,9},{9,8},{10,11... | collective-permute-start | bytes 6291464 | tf_op jit(solution)/shard_map/ppermute | solution.py:397
  19.2 35.8 %collective-permute-start.7 = (bf16[512,1024]{1,0:T(8,128)(2,1)}, bf16[512,1024]{1,0:T(8,128)(2,1)}, u32[]{:S(2)}, u32[]{:S(2)}) collective-permute-start(bf16[512,1024]{1,0:T(8,128)(2,1)} %get-tuple-element.14), channel_id=1, source_target_pairs={{9,0},{7,1},{122,2},{0,3},{11,4},{13,5},{14,6},{4,7},{17,8},{15,9}... | collective-permute-start | bytes 3145736 | tf_op jit(solution)/shard_map/ppermute | solution.py:389
  32.0 23.0 %collective-permute-start.6 = (bf16[512,1024]{1,0:T(8,128)(2,1)}, bf16[512,1024]{1,0:T(8,128)(2,1)}, u32[]{:S(2)}, u32[]{:S(2)}) collective-permute-start(bf16[512,1024]{1,0:T(8,128)(2,1)} %get-tuple-element.14), channel_id=1, source_target_pairs={{6,0},{8,1},{1,2},{123,3},{10,4},{12,5},{127,6},{125,7},{14,8},{16... | collective-permute-start | bytes 3145736 | tf_op jit(solution)/shard_map/ppermute | solution.py:389
  36.0 1.0 copy-start.1
  36.0 29.6 %collective-permute-start.5 = (bf16[512,1024]{1,0:T(8,128)(2,1)}, bf16[512,1024]{1,0:T(8,128)(2,1)}, u32[]{:S(2)}, u32[]{:S(2)}) collective-permute-start(bf16[512,1024]{1,0:T(8,128)(2,1)} %get-tuple-element.14), channel_id=1, source_target_pairs={{3,0},{2,1},{124,2},{5,3},{6,4},{7,5},{0,6},{1,7},{11,8},{10,9},{4... | collective-permute-start | bytes 3145736 | tf_op jit(solution)/shard_map/ppermute | solution.py:389
  36.9 1.0 copy-start.3
  37.9 6.4 %copy-start = (bf16[1024,1024]{1,0:T(8,128)(2,1)S(1)}, bf16[1024,1024]{1,0:T(8,128)(2,1)}, u32[]{:S(2)}) copy-start(bf16[1024,1024]{1,0:T(8,128)(2,1)} %get-tuple-element.11.own_ref) | copy-start | bytes 6291460
  39.0 9.7 %collective-permute-start.4 = (bf16[512,1024]{1,0:T(8,128)(2,1)}, bf16[512,1024]{1,0:T(8,128)(2,1)}, u32[]{:S(2)}, u32[]{:S(2)}) collective-permute-start(bf16[512,1024]{1,0:T(8,128)(2,1)} %select_select_fusion.1), channel_id=1, source_target_pairs={{0,1},{1,0},{2,3},{3,2},{4,5},{5,4},{6,7},{7,6},{8,9},{9,8},{10,11... | collective-permute-start | bytes 3145736 | tf_op jit(solution)/shard_map/ppermute | solution.py:407
  43.4 5.4 %copy-start.2 = (bf16[512,1024]{1,0:T(8,128)(2,1)S(1)}, bf16[512,1024]{1,0:T(8,128)(2,1)}, u32[]{:S(2)}) copy-start(bf16[512,1024]{1,0:T(8,128)(2,1)} %copy-done.1) | copy-start | bytes 3145732
  43.4 5.4 %copy-start.4 = (bf16[512,1024]{1,0:T(8,128)(2,1)S(1)}, bf16[512,1024]{1,0:T(8,128)(2,1)}, u32[]{:S(2)}) copy-start(bf16[512,1024]{1,0:T(8,128)(2,1)} %copy-done.3) | copy-start | bytes 3145732
  66.9 3.2 %collective-permute-start.8 = (bf16[512,1024]{1,0:T(8,128)(2,1)S(1)}, bf16[512,1024]{1,0:T(8,128)(2,1)S(1)}, u32[]{:S(2)}, u32[]{:S(2)}) collective-permute-start(bf16[512,1024]{1,0:T(8,128)(2,1)S(1)} %select_select_fusion), channel_id=1, source_target_pairs={{0,1},{1,0},{2,3},{3,2},{4,5},{5,4},{6,7},{7,6},{8,9},{9,8},{10,11... | collective-permute-start | bytes 3145736 | tf_op jit(solution)/shard_map/ppermute | solution.py:407

commit v4 on v3

--- a/solution.py
+++ b/solution.py
@@ -221,13 +221,17 @@
     work.finish(0, out_ref)
 
 
+def near(step):
+    return 3 if step == len(CHUNKS) - 1 else 2
+
+
 def step_kernel(step, clusters, info_ref, idr_ref, own_ref, sib_ref, *refs):
     last = step == len(CHUNKS) - 1
     new, old, refs = refs[:4], refs[4 : 4 + 4 * step], refs[4 + 4 * step :]
     if last:
         idn_ref, earlier, refs = refs[0], refs[1 : 2 + step], refs[2 + step :]
-    out_ref, idc, accr, accc, data, sems = refs[:6]
-    found = refs[6] if last else out_ref
+    out_ref, idc, accr, accc, data, sib, sems = refs[:7]
+    found = refs[7] if last else out_ref
     first, size = EDGES[step], CHUNKS[step]
     copies = [
         pltpu.make_async_copy(
@@ -238,11 +242,16 @@
         for s in range(4)
         for k in range(step)
     ]
-    for c in copies:
+    newest = [
+        pltpu.make_async_copy(new[s], data.at[pl.ds(s * ROWS + first, size)], sems.at[1])
+        for s in range(4)
+        if s != near(step)
+    ]
+    beside = pltpu.make_async_copy(sib_ref, sib, sems.at[2])
+    for c in newest + [beside] + copies:
         c.start()
-    for s in range(4):
-        at = s * ROWS + first
-        data[at : at + size, :] = new[s][...]
+    at = near(step) * ROWS + first
+    data[at : at + size, :] = new[near(step)][...]
     work = Work(info_ref, idr_ref, idc, accr, accc)
     table = 16 * SLOTS + SLOTS
 
@@ -281,12 +290,15 @@
         return 0
 
     ends = [info_ref[table + i] for i in range(3)]
+    for c in newest:
+        c.wait()
     lax.fori_loop(0, ends[0], own_tiles(own_ref, 0), 0)
-    lax.fori_loop(ends[0], ends[1], own_tiles(sib_ref, 1), 0)
+    beside.wait()
+    lax.fori_loop(ends[0], ends[1], own_tiles(sib, 1), 0)
     if step == 0:
         half = ROWS // 2
         core = lax.rem(info_ref[16 * SLOTS], 2)
-        for c, (left, right) in enumerate(((own_ref, sib_ref), (sib_ref, own_ref))):
+        for c, (left, right) in enumerate(((own_ref, sib), (sib, own_ref))):
 
             @pl.when((core == c) & work.shares(c, c * half, half, 1 - c, 0, ROWS))
             def _(c=c, left=left, right=right):
@@ -357,10 +369,12 @@
     return pl.pallas_call(
         functools.partial(step_kernel, step, clusters),
         out_shape=out,
-        in_specs=[SMEM] + [VMEM] * 7 + [HBM] * len(old) + [VMEM] * len(extra),
+        in_specs=[SMEM, VMEM, VMEM, HBM]
+        + [VMEM if s == near(step) else HBM for s in range(4)]
+        + [HBM] * len(old) + [VMEM] * len(extra),
         out_specs=VMEM,
         scratch_shapes=scratch(SLOTS, SLOTS - 1)
-        + [pltpu.VMEM((4 * ROWS, WIDTH), jnp.bfloat16), pltpu.SemaphoreType.DMA((1,))]
+        + [pltpu.VMEM((4 * ROWS, WIDTH), jnp.bfloat16), pltpu.VMEM((ROWS, WIDTH), jnp.bfloat16), pltpu.SemaphoreType.DMA((3,))]
         + ([pltpu.VMEM((SLOTS, 8, 128), jnp.float32)] if last else []),
         compiler_params=PARAMS,
     )(info, idr, own, sibling, *new, *old, *extra)

time: 108 us -> 108 us (level)
  Pallas kernels: 25.4 us -> 33.9 us
  blocking collectives: 30.2 us -> 25.2 us
  waiting for transfers between devices: 22.9 us -> 20.5 us
    pallas_call x2, Pallas kernels: 13.3 us -> 21.7 us  [step_maxima(): pl.pallas_call(functools.partial(step_kernel, step, clusters), out_shape=...]
    all_to_all x1, blocking collectives: 30.2 us -> 25.2 us  [local(): back = lax.all_to_all(result, AXIS, 0, 0, tiled=True)]
    ppermute x6, waiting for transfers between devices: 20.7 us -> 18.2 us  [send(): return [lax.ppermute(part, AXIS, way) for way in ways]]
  transfers between devices with their start and end apart: 9 -> 9, of which waited for: 5 -> 5; matrix products, arithmetic and copies ran while one was open for 4% -> 4% of each run, Pallas kernels for 14% -> 16%
where the time goes in v4:
time: 108 us; the launch traced here: 110 us
  Pallas kernels  33.9 us (31%)
  blocking collectives  25.2 us (23%)
  waiting for transfers between devices  20.5 us (19%)
  starting transfers between devices  20.1 us (19%)
  other arithmetic  5.3 us (5%)
  local copies, waits for them, and re-layouts  2.8 us (3%)
  between operations  2.07 us (2%)
    all_to_all x1, blocking collectives, local(): back = lax.all_to_all(result, AXIS, 0, 0, tiled=True)  25.2 us
    pallas_call x2, Pallas kernels, step_maxima(): pl.pallas_call(functools.partial(step_kernel, step, clusters), out_shape=...  21.7 us
    ppermute x6, waiting for transfers between devices, send(): return [lax.ppermute(part, AXIS, way) for way in ways]  18.2 us
    ppermute x6, starting transfers between devices, send(): return [lax.ppermute(part, AXIS, way) for way in ways]  11.7 us
    pallas_call x1, Pallas kernels, normalize_all(): pl.pallas_call(norm_all_kernel, out_shape=[jax.ShapeDtypeStruct((ROWS, WI...  4.9 us
    ppermute x2, starting transfers between devices, local(): got[step].append(lax.ppermute(passed, AXIS, swap))  4.55 us
    pallas_call x1, Pallas kernels, own_maxima(): pl.pallas_call(own_kernel, out_shape=maxima(1), in_specs=[SMEM, VMEM, VME...  4.38 us
    ppermute x1, starting transfers between devices, local(): sibling = lax.ppermute(own, AXIS, swap)  3.86 us
  transfers between devices with their start and end apart: 9, of which 5 were waited for; matrix products, arithmetic and copies ran while one was open for 4% of the time, Pallas kernels for 16%

profile of v4, /device:TPU:1, one launch (start us, length us, event | category | flops | bytes accessed | tf_op | source)
XLA Modules:
  0.0 109.8 jit_solution(18277786012642370907)
XLA Ops:
  0.7 2.9 %shard_map.77 = bf16[512,1024]{1,0:T(8,128)(2,1)} custom-call(bf16[1024,1024]{1,0:T(8,128)(2,1)} %x_ref.2), custom_call_target="tpu_custom_call" | custom-call | tf_op jit(solution)/shard_map/pallas_call | solution.py:114
  3.5 6.3 %collective-permute-start.3 = (bf16[512,1024]{1,0:T(8,128)(2,1)}, bf16[512,1024]{1,0:T(8,128)(2,1)S(1)}, u32[]{:S(2)}, u32[]{:S(2)}) collective-permute-start(bf16[512,1024]{1,0:T(8,128)(2,1)} %shard_map.77), channel_id=1, source_target_pairs={{9,0},{7,1},{122,2},{0,3},{11,4},{13,5},{14,6},{4,7},{17,8},{15,9}... | collective-permute-start | bytes 3145736 | tf_op jit(solution)/shard_map/ppermute | solution.py:403
  9.8 0.6 collective-permute-start.1
  10.4 4.9 %shard_map.78 = (bf16[1024,1024]{1,0:T(8,128)(2,1)}, bf16[512,1024]{1,0:T(8,128)(2,1)}) custom-call(bf16[1024,1024]{1,0:T(8,128)(2,1)} %x_ref.2), custom_call_target="tpu_custom_call" | custom-call | tf_op jit(solution)/shard_map/pallas_call | solution.py:142
  15.3 3.9 %collective-permute-start = (bf16[1024,1024]{1,0:T(8,128)(2,1)}, bf16[1024,1024]{1,0:T(8,128)(2,1)}, u32[]{:S(2)}, u32[]{:S(2)}) collective-permute-start(bf16[1024,1024]{1,0:T(8,128)(2,1)} %get-tuple-element.11.own_ref), channel_id=1, source_target_pairs={{0,1},{1,0},{2,3},{3,2},{4,5},{5,4},{6,7},{7,6},{8,9},{9,8},{10,11... | collective-permute-start | bytes 6291464 | tf_op jit(solution)/shard_map/ppermute | solution.py:411
  19.2 4.8 %collective-permute-start.7 = (bf16[512,1024]{1,0:T(8,128)(2,1)}, bf16[512,1024]{1,0:T(8,128)(2,1)}, u32[]{:S(2)}, u32[]{:S(2)}) collective-permute-start(bf16[512,1024]{1,0:T(8,128)(2,1)} %get-tuple-element.14), channel_id=1, source_target_pairs={{9,0},{7,1},{122,2},{0,3},{11,4},{13,5},{14,6},{4,7},{17,8},{15,9}... | collective-permute-start | bytes 3145736 | tf_op jit(solution)/shard_map/ppermute | solution.py:403
  24.0 0.6 dynamic_slice.14
  26.2 0.7 broadcast_multiply_fusion.1
  26.9 5.1 %collective-permute-done.3.refs_2_.refs_6_ = bf16[512,1024]{1,0:T(8,128)(2,1)S(1)} collective-permute-done((bf16[512,1024]{1,0:T(8,128)(2,1)}, bf16[512,1024]{1,0:T(8,128)(2,1)S(1)}, u32[]{:S(2)}, u32[]{:S(2)}) %collective-permute-start.3) | collective-permute-done | bytes 1048608 | tf_op jit(solution)/shard_map/ppermute | solution.py:403
  32.0 4.0 %collective-permute-done.2.refs_1_.refs_5_ = bf16[512,1024]{1,0:T(8,128)(2,1)S(1)} collective-permute-done((bf16[512,1024]{1,0:T(8,128)(2,1)}, bf16[512,1024]{1,0:T(8,128)(2,1)S(1)}, u32[]{:S(2)}, u32[]{:S(2)}) %collective-permute-start.2) | collective-permute-done | bytes 1048608 | tf_op jit(solution)/shard_map/ppermute | solution.py:403
  36.0 1.0 collective-permute-done.1.refs_0_.refs_4_
  36.9 1.0 copy-done.3
  37.9 1.1 %select_select_fusion.1 = bf16[512,1024]{1,0:T(8,128)(2,1)} fusion(bf16[512,1024]{1,0:T(8,128)(2,1)} %copy-done.1, bf16[512,1024]{1,0:T(8,128)(2,1)S(1)} %collective-permute-done.3.refs_2_.refs_6_, bf16[512,1024]{1,0:T(8,128)(2,1)} %copy-done.3, pred[]{:T(512)} %bitcast.5, pred[]{:T(512)} %bitcast.4), kind=kLoop, calls=%fused_computation.2 | loop fusion | flops 1048576 | bytes 4194306 | tf_op jit(solution)/shard_map/jit(_where)/select_n | solution.py:419
  39.0 3.7 %collective-permute-start.4 = (bf16[512,1024]{1,0:T(8,128)(2,1)}, bf16[512,1024]{1,0:T(8,128)(2,1)}, u32[]{:S(2)}, u32[]{:S(2)}) collective-permute-start(bf16[512,1024]{1,0:T(8,128)(2,1)} %select_select_fusion.1), channel_id=1, source_target_pairs={{0,1},{1,0},{2,3},{3,2},{4,5},{5,4},{6,7},{7,6},{8,9},{9,8},{10,11... | collective-permute-start | bytes 3145736 | tf_op jit(solution)/shard_map/ppermute | solution.py:421
  43.4 0.8 dynamic-slice_bitcast_fusion
  44.3 4.4 %shard_map.79.refs_9_ = f32[1,8,128]{2,1,0:T(8,128)S(1)} custom-call(s32[123]{0:T(128)S(1)} %pad_add_fusion.1.info_ref, bf16[1024,1024]{1,0:T(8,128)(2,1)S(1)} %copy-done, f32[1,1,1024]{2,1,0:T(1,128)S(1)} %slice_bitcast_fusion.idr_ref), custom_call_target="tpu_custom_call" | custom-call | tf_op jit(solution)/shard_map/pallas_call | solution.py:355
  48.8 8.6 %shard_map.80.refs_10_ = f32[6,8,128]{2,1,0:T(8,128)S(1)} custom-call(s32[123]{0:T(128)S(1)} %pad_add_fusion.1.info_ref, f32[6,1,1024]{2,1,0:T(1,128)S(1)} %convert_element_type.23.idr_ref, bf16[1024,1024]{1,0:T(8,128)(2,1)S(1)} %copy-done, bf16[1024,1024]{1,0:T(8,128)(2,1)} %collective-permute-done.sib_ref, bf16[512,1024]{1,0:T(8,128)(2,1)S(1)} %copy-done.4, ...), custom_call_target="tpu_custom_call" | custom-call | tf_op jit(solution)/shard_map/pallas_call | solution.py:369
  57.4 8.1 %collective-permute-done.5.refs_0_ = bf16[512,1024]{1,0:T(8,128)(2,1)} collective-permute-done((bf16[512,1024]{1,0:T(8,128)(2,1)}, bf16[512,1024]{1,0:T(8,128)(2,1)}, u32[]{:S(2)}, u32[]{:S(2)}) %collective-permute-start.5) | collective-permute-done | bytes 1048608 | tf_op jit(solution)/shard_map/ppermute | solution.py:403
  65.6 1.4 %select_select_fusion = bf16[512,1024]{1,0:T(8,128)(2,1)S(1)} fusion(bf16[512,1024]{1,0:T(8,128)(2,1)} %collective-permute-done.6.refs_1_, bf16[512,1024]{1,0:T(8,128)(2,1)} %collective-permute-done.7.refs_2_, bf16[512,1024]{1,0:T(8,128)(2,1)} %collective-permute-done.5.refs_0_, pred[]{:T(512)} %bitcast.5, pred[]{:T(512)} %bitcast.4), kind=kLoop, calls=%fused_computation.1 | loop fusion | flops 1048576 | bytes 4194306 | tf_op jit(solution)/shard_map/jit(_where)/select_n | solution.py:419
  66.9 0.9 collective-permute-start.8
  67.8 2.3 %collective-permute-done.8.refs_3_ = bf16[512,1024]{1,0:T(8,128)(2,1)S(1)} collective-permute-done((bf16[512,1024]{1,0:T(8,128)(2,1)S(1)}, bf16[512,1024]{1,0:T(8,128)(2,1)S(1)}, u32[]{:S(2)}, u32[]{:S(2)}) %collective-permute-start.8) | collective-permute-done | bytes 1048608 | tf_op jit(solution)/shard_map/ppermute | solution.py:421
  70.1 13.1 %shard_map.81 = f32[128,9,128]{2,1,0:T(8,128)S(1)} custom-call(s32[123]{0:T(128)S(1)} %pad_add_fusion.1.info_ref, f32[6,1,1024]{2,1,0:T(1,128)S(1)} %convert_element_type.23.idr_ref, bf16[1024,1024]{1,0:T(8,128)(2,1)S(1)} %copy-done, bf16[1024,1024]{1,0:T(8,128)(2,1)} %collective-permute-done.sib_ref, bf16[512,1024]{1,0:T(8,128)(2,1)} %collective-permute-done.5.refs_0_, ...), custom_call_target="tpu_custom_call" | custom-call | tf_op jit(solution)/shard_map/pallas_call | solution.py:369
  83.2 25.2 %all_to_all.5 = f32[128,9,128]{2,1,0:T(8,128)S(1)} all-to-all(f32[128,9,128]{2,1,0:T(8,128)S(1)} %shard_map.81), channel_id=1, replica_groups=mesh['docs'=128] {'docs'}, dimensions={0} | all-to-all | bytes 1179648 | tf_op jit(solution)/shard_map/all_to_all | solution.py:431
  108.5 0.6 multiply_bitcast_fusion
  (37 shorter events, 1.9 us)
Async XLA Ops:
  0.6 23.3 %copy-start.6 = (s32[8]{0:T(128)S(1)}, s32[8]{0:T(128)}, u32[]{:S(2)}) copy-start(s32[8]{0:T(128)} %constant.53.clone) | copy-start | bytes 100
  0.6 25.2 %copy-start.5 = (s32[64]{0:T(128)S(1)}, s32[64]{0:T(128)}, u32[]{:S(2)}) copy-start(s32[64]{0:T(128)} %param.7) | copy-start | bytes 772
  3.5 28.5 %collective-permute-start.3 = (bf16[512,1024]{1,0:T(8,128)(2,1)}, bf16[512,1024]{1,0:T(8,128)(2,1)S(1)}, u32[]{:S(2)}, u32[]{:S(2)}) collective-permute-start(bf16[512,1024]{1,0:T(8,128)(2,1)} %shard_map.77), channel_id=1, source_target_pairs={{9,0},{7,1},{122,2},{0,3},{11,4},{13,5},{14,6},{4,7},{17,8},{15,9}... | collective-permute-start | bytes 3145736 | tf_op jit(solution)/shard_map/ppermute | solution.py:403
  9.8 26.1 %collective-permute-start.2 = (bf16[512,1024]{1,0:T(8,128)(2,1)}, bf16[512,1024]{1,0:T(8,128)(2,1)S(1)}, u32[]{:S(2)}, u32[]{:S(2)}) collective-permute-start(bf16[512,1024]{1,0:T(8,128)(2,1)} %shard_map.77), channel_id=1, source_target_pairs={{6,0},{8,1},{1,2},{123,3},{10,4},{12,5},{127,6},{125,7},{14,8},{16... | collective-permute-start | bytes 3145736 | tf_op jit(solution)/shard_map/ppermute | solution.py:403
  9.8 27.1 %collective-permute-start.1 = (bf16[512,1024]{1,0:T(8,128)(2,1)}, bf16[512,1024]{1,0:T(8,128)(2,1)S(1)}, u32[]{:S(2)}, u32[]{:S(2)}) collective-permute-start(bf16[512,1024]{1,0:T(8,128)(2,1)} %shard_map.77), channel_id=1, source_target_pairs={{3,0},{2,1},{124,2},{5,3},{6,4},{7,5},{0,6},{1,7},{11,8},{10,9},{4... | collective-permute-start | bytes 3145736 | tf_op jit(solution)/shard_map/ppermute | solution.py:403
  15.3 33.4 %collective-permute-start = (bf16[1024,1024]{1,0:T(8,128)(2,1)}, bf16[1024,1024]{1,0:T(8,128)(2,1)}, u32[]{:S(2)}, u32[]{:S(2)}) collective-permute-start(bf16[1024,1024]{1,0:T(8,128)(2,1)} %get-tuple-element.11.own_ref), channel_id=1, source_target_pairs={{0,1},{1,0},{2,3},{3,2},{4,5},{5,4},{6,7},{7,6},{8,9},{9,8},{10,11... | collective-permute-start | bytes 6291464 | tf_op jit(solution)/shard_map/ppermute | solution.py:411
  19.2 38.2 %collective-permute-start.7 = (bf16[512,1024]{1,0:T(8,128)(2,1)}, bf16[512,1024]{1,0:T(8,128)(2,1)}, u32[]{:S(2)}, u32[]{:S(2)}) collective-permute-start(bf16[512,1024]{1,0:T(8,128)(2,1)} %get-tuple-element.14), channel_id=1, source_target_pairs={{9,0},{7,1},{122,2},{0,3},{11,4},{13,5},{14,6},{4,7},{17,8},{15,9}... | collective-permute-start | bytes 3145736 | tf_op jit(solution)/shard_map/ppermute | solution.py:403
  32.0 25.4 %collective-permute-start.6 = (bf16[512,1024]{1,0:T(8,128)(2,1)}, bf16[512,1024]{1,0:T(8,128)(2,1)}, u32[]{:S(2)}, u32[]{:S(2)}) collective-permute-start(bf16[512,1024]{1,0:T(8,128)(2,1)} %get-tuple-element.14), channel_id=1, source_target_pairs={{6,0},{8,1},{1,2},{123,3},{10,4},{12,5},{127,6},{125,7},{14,8},{16... | collective-permute-start | bytes 3145736 | tf_op jit(solution)/shard_map/ppermute | solution.py:403
  36.0 1.0 copy-start.1
  36.0 29.6 %collective-permute-start.5 = (bf16[512,1024]{1,0:T(8,128)(2,1)}, bf16[512,1024]{1,0:T(8,128)(2,1)}, u32[]{:S(2)}, u32[]{:S(2)}) collective-permute-start(bf16[512,1024]{1,0:T(8,128)(2,1)} %get-tuple-element.14), channel_id=1, source_target_pairs={{3,0},{2,1},{124,2},{5,3},{6,4},{7,5},{0,6},{1,7},{11,8},{10,9},{4... | collective-permute-start | bytes 3145736 | tf_op jit(solution)/shard_map/ppermute | solution.py:403
  36.9 1.0 copy-start.3
  37.9 6.4 %copy-start = (bf16[1024,1024]{1,0:T(8,128)(2,1)S(1)}, bf16[1024,1024]{1,0:T(8,128)(2,1)}, u32[]{:S(2)}) copy-start(bf16[1024,1024]{1,0:T(8,128)(2,1)} %get-tuple-element.11.own_ref) | copy-start | bytes 6291460
  39.0 9.7 %collective-permute-start.4 = (bf16[512,1024]{1,0:T(8,128)(2,1)}, bf16[512,1024]{1,0:T(8,128)(2,1)}, u32[]{:S(2)}, u32[]{:S(2)}) collective-permute-start(bf16[512,1024]{1,0:T(8,128)(2,1)} %select_select_fusion.1), channel_id=1, source_target_pairs={{0,1},{1,0},{2,3},{3,2},{4,5},{5,4},{6,7},{7,6},{8,9},{9,8},{10,11... | collective-permute-start | bytes 3145736 | tf_op jit(solution)/shard_map/ppermute | solution.py:421
  43.4 5.4 %copy-start.2 = (bf16[512,1024]{1,0:T(8,128)(2,1)S(1)}, bf16[512,1024]{1,0:T(8,128)(2,1)}, u32[]{:S(2)}) copy-start(bf16[512,1024]{1,0:T(8,128)(2,1)} %copy-done.1) | copy-start | bytes 3145732
  43.4 5.4 %copy-start.4 = (bf16[512,1024]{1,0:T(8,128)(2,1)S(1)}, bf16[512,1024]{1,0:T(8,128)(2,1)}, u32[]{:S(2)}) copy-start(bf16[512,1024]{1,0:T(8,128)(2,1)} %copy-done.3) | copy-start | bytes 3145732
  66.9 3.2 %collective-permute-start.8 = (bf16[512,1024]{1,0:T(8,128)(2,1)S(1)}, bf16[512,1024]{1,0:T(8,128)(2,1)S(1)}, u32[]{:S(2)}, u32[]{:S(2)}) collective-permute-start(bf16[512,1024]{1,0:T(8,128)(2,1)S(1)} %select_select_fusion), channel_id=1, source_target_pairs={{0,1},{1,0},{2,3},{3,2},{4,5},{5,4},{6,7},{7,6},{8,9},{9,8},{10,11... | collective-permute-start | bytes 3145736 | tf_op jit(solution)/shard_map/ppermute | solution.py:421
